TPU v7x, 256 devices: a whole 4x4x8 slice. The times are simulated.
256 devices in a mesh: dp: 32 (over x, z), tensor: 8 (over y, core).
Axes of the slice: x: 4, y: 4, z: 8, core: 2. Of those that a mesh axis runs over, the one named last changes fastest.
Arguments:
- q_lat: bfloat16 [1024, 65536], P('dp', 'tensor'), may hold values from -48 to 48
- q_rope: bfloat16 [1024, 8192], P('dp', 'tensor'), may hold values from -6 to 6
- fresh_lat: bfloat16 [1024, 512], P('dp'), may hold values from -4 to 4
- fresh_rope: bfloat16 [1024, 64], P('dp'), may hold values from -6 to 6
- cache_lat: bfloat16 [2048, 128, 512], P('dp'), may hold values from -6 to 6
- cache_rope: bfloat16 [2048, 64, 128], P('dp'), may hold values from -6 to 6
- page_table: int32 [32, 2, 32], P('dp'), may hold values from 0 to 63, as said below
- hit_len: int32 [32, 2], P('dp'), may hold values from 1 to 4096, as said below
- fresh_len: int32 [32, 2], P('dp'), may hold values from 1 to 24, 32 in all within a row
- w_uv: bfloat16 [128, 512, 128], P('tensor'), may hold values from -0.25 to 0.25
- w_o: bfloat16 [16384, 7168], P('tensor', 'dp'), may hold values from -0.046875 to 0.046875
- resid: bfloat16 [1024, 7168], P('tensor', 'dp'), may hold values from -5 to 5
- norm_gain: bfloat16 [7168], P('dp'), may hold values from 0.099609375 to 1.8984375
- w_gate: bfloat16 [7168, 18432], P('dp', 'tensor'), may hold values from -0.0625 to 0.0625
- w_up: bfloat16 [7168, 18432], P('dp', 'tensor'), may hold values from -0.0625 to 0.0625
- w_down: bfloat16 [18432, 7168], P('tensor', 'dp'), may hold values from -0.046875 to 0.046875
Outputs:
- mixed: bfloat16 [1024, 7168], P('tensor', 'dp')
Inputs may be any that keep to these rules, and one draw needn't show every extreme that they name: `page_table`: each group's row of the table lists every number from 0 to 63 once. `hit_len`: some request of some group has the full 32 * 128 cached tokens. `fresh_len`: each group's counts sum to 32.
All inputs are finite; a program needn't handle non-finite values.
Results may differ from a plain program's by a relative error of at most 0.025.
Values may be sent and summed in bfloat16 or wider, within the bound.
A program may use at most 128 MiB of HBM per device.

v0:
```python
import jax
import jax.numpy as jnp
from jax import lax
from jax.sharding import PartitionSpec as P

D = 7168
ROPE = 64
VDIM = 128


epsilon = 1e-06


def attend_local(
    q_lat,
    q_rope,
    fresh_lat,
    fresh_rope,
    cache_lat,
    cache_rope,
    page_table,
    hit_len,
    fresh_len,
    w_uv,
):
    heads, latent_width, value_width = w_uv.shape
    rows_here = fresh_lat.shape[0]
    queries = q_lat.reshape(rows_here, heads, latent_width)
    rope_query = q_rope.reshape(rows_here, heads, fresh_rope.shape[1])
    order = page_table[0].reshape(-1)
    keys_lat = cache_lat[order].reshape(-1, latent_width)
    keys_rope = jnp.transpose(cache_rope[order], (1, 0, 2)).reshape(cache_rope.shape[1], -1)
    counts = fresh_len[0]
    hit = hit_len[0]
    row_ids = jnp.arange(rows_here, dtype=jnp.int32)
    bounds = jnp.cumsum(counts)[:-1]
    row_request = jnp.sum((row_ids[:, None] >= bounds[None, :]).astype(jnp.int32), axis=1)
    key_ids = jnp.arange(keys_lat.shape[0], dtype=jnp.int32)
    span_len = keys_lat.shape[0] // counts.shape[0]
    key_request = key_ids // span_len
    key_place = key_ids % span_len
    request_ids = jnp.arange(counts.shape[0], dtype=jnp.int32)
    limits = jnp.sum(
        jnp.where(key_request[:, None] == request_ids[None, :], hit[None, :], 0), axis=1
    )
    cache_mask = (row_request[:, None] == key_request[None, :]) & (
        key_place[None, :] < limits[None, :]
    )
    fresh_mask = (row_request[:, None] == row_request[None, :]) & (
        row_ids[None, :] <= row_ids[:, None]
    )
    factor = (VDIM + ROPE) ** (-0.5)
    cache_scores = factor * (
        jnp.einsum("rhl,kl->rhk", queries, keys_lat, preferred_element_type=jnp.float32)
        + jnp.einsum("rhe,ek->rhk", rope_query, keys_rope, preferred_element_type=jnp.float32)
    )
    fresh_scores = factor * (
        jnp.einsum("rhl,jl->rhj", queries, fresh_lat, preferred_element_type=jnp.float32)
        + jnp.einsum("rhe,je->rhj", rope_query, fresh_rope, preferred_element_type=jnp.float32)
    )
    cache_scores = jnp.where(cache_mask[:, None, :], cache_scores, -jnp.inf)
    fresh_scores = jnp.where(fresh_mask[:, None, :], fresh_scores, -jnp.inf)
    peak = jnp.maximum(jnp.max(cache_scores, axis=2), jnp.max(fresh_scores, axis=2))
    cache_exp = jnp.exp(cache_scores - peak[..., None])
    fresh_exp = jnp.exp(fresh_scores - peak[..., None])
    denominator = jnp.sum(cache_exp, axis=2) + jnp.sum(fresh_exp, axis=2)
    cache_weights = (cache_exp / denominator[..., None]).astype(jnp.bfloat16)
    fresh_weights = (fresh_exp / denominator[..., None]).astype(jnp.bfloat16)
    latent_out = (
        jnp.einsum("rhk,kl->rhl", cache_weights, keys_lat, preferred_element_type=jnp.float32)
        + jnp.einsum("rhj,jl->rhl", fresh_weights, fresh_lat, preferred_element_type=jnp.float32)
    ).astype(jnp.bfloat16)
    values = jnp.einsum(
        "rhl,hlv->rhv", latent_out, w_uv, preferred_element_type=jnp.float32
    ).astype(jnp.bfloat16)
    return values.reshape(rows_here, heads * value_width)


def local(
    q_lat,
    q_rope,
    fresh_lat,
    fresh_rope,
    cache_lat,
    cache_rope,
    page_table,
    hit_len,
    fresh_len,
    w_uv,
    w_o,
    resid,
    norm_gain,
    w_gate,
    w_up,
    w_down,
):
    head_values = attend_local(
        q_lat,
        q_rope,
        fresh_lat,
        fresh_rope,
        cache_lat,
        cache_rope,
        page_table,
        hit_len,
        fresh_len,
        w_uv,
    )
    attn_terms = jnp.dot(
        lax.all_gather(head_values, "dp", axis=0, tiled=True),
        w_o,
        preferred_element_type=jnp.float32,
    )
    gain_f = norm_gain.astype(jnp.float32)
    attn_part = lax.psum_scatter(
        attn_terms.astype(jnp.bfloat16), "tensor", scatter_dimension=0, tiled=True
    ).astype(jnp.float32)
    stream = resid.astype(jnp.float32) + attn_part
    squares = lax.psum(jnp.sum(stream * stream, axis=1), "dp")
    normed = (stream * lax.rsqrt(squares[:, None] / D + epsilon) * gain_f).astype(jnp.bfloat16)
    all_normed = lax.all_gather(normed, "tensor", axis=0, tiled=True)
    gate_terms = jnp.dot(all_normed, w_gate, preferred_element_type=jnp.float32)
    up_terms = jnp.dot(all_normed, w_up, preferred_element_type=jnp.float32)
    gate_pre, up_pre = (
        lax.psum_scatter(
            gate_terms.astype(jnp.bfloat16), "dp", scatter_dimension=0, tiled=True
        ).astype(jnp.float32),
        lax.psum_scatter(
            up_terms.astype(jnp.bfloat16), "dp", scatter_dimension=0, tiled=True
        ).astype(jnp.float32),
    )
    hidden = (jax.nn.silu(gate_pre) * up_pre).astype(jnp.bfloat16)
    down_terms = jnp.dot(
        lax.all_gather(hidden, "dp", axis=0, tiled=True), w_down, preferred_element_type=jnp.float32
    )
    mlp_part = lax.psum_scatter(
        down_terms.astype(jnp.bfloat16), "tensor", scatter_dimension=0, tiled=True
    ).astype(jnp.float32)
    return (stream + mlp_part).astype(jnp.bfloat16)


def solution(mesh):
    placed = (
        P("dp", "tensor"),
        P("dp", "tensor"),
        P("dp", None),
        P("dp", None),
        P("dp", None, None),
        P("dp", None, None),
        P("dp", None, None),
        P("dp", None),
        P("dp", None),
        P("tensor", None, None),
        P("tensor", "dp"),
        P("tensor", "dp"),
        P("dp"),
        P("dp", "tensor"),
        P("dp", "tensor"),
        P("tensor", "dp"),
    )
    return jax.shard_map(
        local, mesh=mesh, in_specs=placed, out_specs=P("tensor", "dp"), check_vma=False
    )
```

profile of v0, /device:TPU:1, one launch (start us, length us, event | category | flops | bytes accessed | tf_op | source)
XLA Modules:
  0.0 863.4 jit_solution(11209729577762101769)
XLA Ops:
  6.5 0.0 copy-start
  6.5 0.0 all-gather.3.cloned.1.call-start
  6.5 1.0 fusion.20
  7.5 0.8 reduce-window.4
  8.4 0.1 fusion.33
  8.5 0.2 compare_and_fusion
  8.7 0.8 reshape_squeeze.3
  9.5 2.0 gather_fusion.1
  11.5 1.7 copy.52
  13.2 1.5 reshape.215
  14.7 1.0 reshape.196
  15.7 8.9 %gather_fusion = bf16[64,128,512]{2,1,0:T(8,128)(2,1)} fusion(bf16[64,128,512]{2,1,0:T(8,128)(2,1)} %param.20, s32[1024]{0:T(1024)S(1)} %pad_clamp_fusion), kind=kCustom, calls=%fused_computation | custom fusion | bytes 16777472 | tf_op jit(solution)/shard_map/gather | solution.py:31
  24.6 1.2 copy.70
  25.8 0.0 copy-start.2
  25.8 0.0 copy-start.3
  25.8 8.0 fusion.18
  33.9 0.0 copy-done.2
  33.9 0.3 fusion.31
  34.1 0.0 copy-done.3
  34.1 0.3 fusion.37
  34.4 0.1 copy.56
  34.5 19.1 %fusion.36 = (f32[32,16]{0,1:T(8,128)S(1)}, f32[32,16,8192]{2,0,1:T(8,128)}) fusion(f32[8192,32,16]{0,1,2:T(8,128)} %fusion.18, bf16[8192,512,1]{1,0,2:T(8,128)(2,1)} %bitcast.53, bf16[4,16,8,512]{3,2,1,0:T(8,128)(2,1)} %bitcast.58, pred[32,8192]{1,0:T(8,128)(4,1)S(1)} %compare_and_fusion), kind=kOutput, calls=%fused_computation.65 | convolution fusion | flops 4311744000 | bytes 42731520 | tf_op jit(solution)/shard_map/rhl,kl->rhk/dot_general | solution.py:54
  53.6 0.1 copy.57
  53.7 8.1 fusion
  61.8 0.3 fusion.15
  62.1 0.1 copy.58
  62.1 10.7 %fusion.1 = f32[32,16,512]{2,0,1:T(8,128)S(1)} fusion(bf16[8192,512,1]{1,0,2:T(8,128)(2,1)} %bitcast.54, f32[32,16,8192]{2,0,1:T(8,128)} %get-tuple-element.6, f32[32,16]{0,1:T(8,128)S(1)} %add.78, f32[32,16]{0,1:T(8,128)S(1)} %max.7), kind=kOutput, calls=%fused_computation.6 | convolution fusion | flops 4307550208 | bytes 26218496 | tf_op jit(solution)/shard_map/rhk,kl->rhl/dot_general | solution.py:70
  72.9 0.7 copy.59
  73.5 0.9 divide_convert_fusion.2
  74.5 0.0 copy-done
  74.5 1.3 fusion.7
  75.8 0.7 copy.83
  76.5 0.0 all-gather.3.cloned.1.call-update
  76.5 0.0 reduce-scatter.13.cloned.1.call-start
  76.5 83.0 %all-gather.3.cloned.1.call-done = bf16[1024,2048]{1,0:T(8,128)(2,1)} async-done(((bf16[32,2048]{1,0:T(8,128)(2,1)}), bf16[1024,2048]{1,0:T(8,128)(2,1)}) %all-gather.3.cloned.1.call-update) | async-done | bytes 4194320 | tf_op jit(solution)/shard_map/all_gather | solution.py:110
  159.5 3.9 convolution_convert_fusion.3
  163.4 1.0 copy.64
  164.4 0.0 reduce-scatter.13.cloned.1.call-update
  164.4 0.0 reduce-scatter.11.cloned.1.call-start
  164.5 0.7 convert_element_type.76
  165.2 30.5 %reduce-scatter.13.cloned.1.call-done = bf16[128,224]{1,0:T(8,128)(2,1)} async-done(((bf16[1024,224]{1,0:T(8,128)(2,1)}), bf16[128,224]{1,0:T(8,128)(2,1)}) %reduce-scatter.13.cloned.1.call-update) | async-done | bytes 57360
  195.7 0.9 copy.65
  196.6 0.9 multiply_reduce_fusion
  197.5 61.0 %psum.7 = f32[128]{0:T(128)S(1)} all-reduce(f32[128]{0:T(128)S(1)} %multiply_reduce_fusion), channel_id=1, replica_groups=mesh['dp'=32,'tensor'=8] {'dp'}, use_global_device_ids=true, to_apply=%region_8.9 | all-reduce | flops 128 | bytes 1024 | tf_op jit(solution)/shard_map/psum | solution.py:119
  258.6 0.9 multiply_convert_fusion
  259.5 29.0 %all_gather.10 = bf16[1024,224]{0,1:T(8,128)(2,1)S(1)} all-gather(bf16[128,224]{0,1:T(8,128)(2,1)S(1)} %multiply_convert_fusion), channel_id=1, replica_groups=mesh['dp'=32,'tensor'=8] {'tensor'}, dimensions={0}, use_global_device_ids=true | all-gather | bytes 516096 | tf_op jit(solution)/shard_map/all_gather | solution.py:121
  288.4 4.8 convolution_convert_fusion
  293.2 0.0 reduce-scatter.11.cloned.1.call-update
  293.2 0.0 reduce-scatter.9.cloned.1.call-start
  293.3 4.8 convolution_convert_fusion.1
  298.1 0.0 reduce-scatter.9.cloned.1.call-update
  298.2 0.0 all-gather.5.cloned.1.call-start
  298.2 206.7 %reduce-scatter.11.cloned.1.call-done = bf16[32,2304]{1,0:T(8,128)(2,1)} async-done(((bf16[1024,2304]{1,0:T(8,128)(2,1)}), bf16[32,2304]{1,0:T(8,128)(2,1)}) %reduce-scatter.11.cloned.1.call-update) | async-done | bytes 147472 | tf_op jit(solution)/shard_map/reduce_scatter | solution.py:128
  504.9 227.2 %reduce-scatter.9.cloned.1.call-done = bf16[32,2304]{1,0:T(8,128)(2,1)} async-done(((bf16[1024,2304]{1,0:T(8,128)(2,1)}), bf16[32,2304]{1,0:T(8,128)(2,1)}) %reduce-scatter.9.cloned.1.call-update) | async-done | bytes 147472 | tf_op jit(solution)/shard_map/reduce_scatter | solution.py:125
  732.0 1.7 fusion.14
  733.8 0.0 all-gather.5.cloned.1.call-update
  733.8 0.0 reduce-scatter.15.cloned.1.call-start
  733.8 84.7 %all-gather.5.cloned.1.call-done = bf16[1024,2304]{1,0:T(8,128)(2,1)} async-done(((bf16[32,2304]{1,0:T(8,128)(2,1)}), bf16[1024,2304]{1,0:T(8,128)(2,1)}) %all-gather.5.cloned.1.call-update) | async-done | bytes 4718608 | tf_op jit(solution)/shard_map/all_gather | solution.py:134
  818.5 4.2 convolution_convert_fusion.2
  822.7 1.0 copy.66
  823.7 0.0 reduce-scatter.15.cloned.1.call-update
  823.7 31.2 %reduce-scatter.15.cloned.1.call-done = bf16[128,224]{1,0:T(8,128)(2,1)} async-done(((bf16[1024,224]{1,0:T(8,128)(2,1)}), bf16[128,224]{1,0:T(8,128)(2,1)}) %reduce-scatter.15.cloned.1.call-update) | async-done | bytes 57360
  855.0 0.9 copy.67
  855.9 0.7 add_convert_fusion
  (10 shorter events, 0.1 us)
Async XLA Ops:
  6.5 67.9 %copy-start = (bf16[16,512,128]{2,1,0:T(8,128)(2,1)S(1)}, bf16[16,512,128]{2,1,0:T(8,128)(2,1)}, u32[]{:S(2)}) copy-start(bf16[16,512,128]{2,1,0:T(8,128)(2,1)} %param.25) | copy-start | bytes 6291460
  6.5 153.0 %all-gather.3.cloned.1.call-start = ((), (), s32[]{:S(2)}) async-start(), calls=%async_computation.4 | async-start | bytes 4325376 | tf_op jit(solution)/shard_map/all_gather | solution.py:110
  25.8 8.0 copy-start.2
  25.8 8.3 copy-start.3
  76.5 119.2 %reduce-scatter.13.cloned.1.call-start = ((), (), s32[]{:S(2)}) async-start(), calls=%async_computation.8 | async-start | bytes 589824
  164.4 340.4 %reduce-scatter.11.cloned.1.call-start = ((), (), s32[]{:S(2)}) async-start(), calls=%async_computation.6 | async-start | bytes 4866048 | tf_op jit(solution)/shard_map/reduce_scatter | solution.py:128
  293.2 438.8 %reduce-scatter.9.cloned.1.call-start = ((), (), s32[]{:S(2)}) async-start(), calls=%async_computation.5 | async-start | bytes 4866048 | tf_op jit(solution)/shard_map/reduce_scatter | solution.py:125
  298.1 557.8 %copy-start.1 = (bf16[128,224]{0,1:T(8,128)(2,1)S(1)}, bf16[128,224]{0,1:T(8,128)(2,1)}, u32[]{:S(2)}) copy-start(bf16[128,224]{0,1:T(8,128)(2,1)} %param.27) | copy-start | bytes 172036
  298.2 520.4 %all-gather.5.cloned.1.call-start = ((), (), s32[]{:S(2)}) async-start(), calls=%async_computation.7 | async-start | bytes 4866048 | tf_op jit(solution)/shard_map/all_gather | solution.py:134
  733.8 121.2 %reduce-scatter.15.cloned.1.call-start = ((), (), s32[]{:S(2)}) async-start(), calls=%async_computation.9 | async-start | bytes 589824
Sparse Core Ops, SparseCore 0:
  76.6 82.8 all-gather.2
  164.6 31.0 reduce-scatter.12
  293.4 211.4 reduce-scatter.10
  509.2 222.8 reduce-scatter.8
  734.8 83.7 all-gather.4
  823.9 31.0 reduce-scatter.14
where the time goes:
time: 866 us; the launch traced here: 863 us
  waiting for transfers between devices  663 us (77%)
  blocking collectives  90 us (10%)
  matrix products  57.4 us (7%)
  local copies, waits for them, and re-layouts  22.5 us (3%)
  other arithmetic  16.3 us (2%)
  between operations  13.7 us (2%)
    reduce_scatter x1, waiting for transfers between devices, local(): lax.psum_scatter(gate_terms.astype(jnp.bfloat16), 'dp', scatter_dimension...  227 us
    reduce_scatter x1, waiting for transfers between devices, local(): lax.psum_scatter(up_terms.astype(jnp.bfloat16), 'dp', scatter_dimension=0...  207 us
    all_gather x1, waiting for transfers between devices, local(): lax.all_gather(hidden, 'dp', axis=0, tiled=True)  84.7 us
    all_gather x1, waiting for transfers between devices, local(): lax.all_gather(head_values, 'dp', axis=0, tiled=True)  83 us
    unnamed x8, waiting for transfers between devices  61.9 us
    psum x1, blocking collectives, local(): squares = lax.psum(jnp.sum(stream * stream, axis=1), 'dp')  61 us
    all_gather x1, blocking collectives, local(): all_normed = lax.all_gather(normed, 'tensor', axis=0, tiled=True)  29 us
    dot_general x1, matrix products, attend_local(): jnp.einsum('rhl,kl->rhk', queries, keys_lat, preferred_element_type=jnp.f...  19.1 us
  transfers between devices with their start and end apart: 6, of which 6 were waited for; matrix products, arithmetic and copies ran while one was open for 1% of the time, Pallas kernels for 0%

commit v1 on v0

--- a/solution.py
+++ b/solution.py
@@ -1,14 +1,20 @@
+import functools
+
 import jax
 import jax.numpy as jnp
 from jax import lax
+from jax.experimental import pallas as pl
+from jax.experimental.pallas import tpu as pltpu
 from jax.sharding import PartitionSpec as P
 
 D = 7168
 ROPE = 64
 VDIM = 128
-
-
-epsilon = 1e-06
+X, Y, Z = 4, 4, 8
+EPS = 1e-06
+MESH = pl.DeviceIdType.MESH
+F32 = jnp.float32
+BF16 = jnp.bfloat16
 
 
 def attend_local(
@@ -73,7 +79,337 @@
     values = jnp.einsum(
         "rhl,hlv->rhv", latent_out, w_uv, preferred_element_type=jnp.float32
     ).astype(jnp.bfloat16)
-    return values.reshape(rows_here, heads * value_width)
+    return jnp.transpose(values.reshape(rows_here, X, -1), (1, 0, 2))
+
+
+def layer_kernel(
+    hv, resid, gain,
+    wgu0, wgu1, wgu2, wgu3, wo0, wo1, wo2, wo3, wd0, wd1, wd2, wd3,
+    out,
+    heads, normed, wgu, part_o, part_d, sib_o, sib_d,
+    a1_o, b1_o, ra_o, rb_o, a2_o, b2_o,
+    a1_d, b1_d, ra_d, rb_d, a2_d, b2_d,
+    terms, from_left, from_right, hidden, stream,
+    ssem, rsem, wsem,
+):
+    dp, tensor = lax.axis_index("dp"), lax.axis_index("tensor")
+    x, z = dp // Z, lax.rem(dp, Z)
+    y, c = tensor // 2, lax.rem(tensor, 2)
+
+    def near(dx=0, dy=0, dz=0, dc=0):
+        return (
+            lax.rem(x + dx, X) * Z + lax.rem(z + dz, Z),
+            lax.rem(y + dy, Y) * 2 + lax.rem(c + dc, 2),
+        )
+
+    x_of = [near(dx=k) for k in range(X)]
+    y_of = [near(dy=k) for k in range(Y)]
+    right, left, sibling = near(dz=1), near(dz=Z - 1), near(dc=1)
+
+    loads = []
+    for s, block in enumerate((wgu0, wgu1, wgu2, wgu3)):
+        row = pl.multiple_of(lax.rem(x - s + X, X) * 256, 256)
+        load = pltpu.make_async_copy(block, wgu.at[pl.ds(row, 224), :], wsem.at[s])
+        load.start()
+        loads.append(load)
+
+    barrier = pltpu.get_barrier_semaphore()
+    partners = x_of[1:] + y_of[1:] + [right, left, sibling]
+    for device in partners:
+        pl.semaphore_signal(barrier, inc=1, device_id=device, device_id_type=MESH)
+    pl.semaphore_wait(barrier, len(partners))
+
+    sent = []
+
+    def send(src, dst, device):
+        at = len(sent)
+        copy = pltpu.make_async_remote_copy(
+            src_ref=src, dst_ref=dst, send_sem=ssem.at[at], recv_sem=rsem.at[at],
+            device_id=device, device_id_type=MESH,
+        )
+        copy.start()
+        sent.append(copy)
+        return copy
+
+    def ring_gather(view, first, arrived):
+        got = {}
+        for sub in range(4):
+            first(sub)
+            piece = view(z, sub)
+            got["r", 0, sub] = send(piece, piece, right)
+            got["l", 0, sub] = send(piece, piece, left)
+        for hop in range(1, 4):
+            zl, zr = lax.rem(z - hop + Z, Z), lax.rem(z + hop, Z)
+            for sub in range(4):
+                got["r", hop - 1, sub].wait_recv()
+                if hop < 3 or sub < 2:
+                    piece = view(zl, sub)
+                    got["r", hop, sub] = send(piece, piece, right)
+                got["l", hop - 1, sub].wait_recv()
+                if hop < 3 or sub >= 2:
+                    piece = view(zr, sub)
+                    got["l", hop, sub] = send(piece, piece, left)
+            arrived(zl)
+            arrived(zr)
+        for sub in range(4):
+            got["r" if sub < 2 else "l", 3, sub].wait_recv()
+        arrived(lax.rem(z + 4, Z))
+
+    def reduce_scatter(part, sib, a1, b1, ra, rb, a2, b2):
+        swaps = []
+        for k in (1, 2, 3, 0):
+            yk = lax.rem(y + k, Y)
+            swaps.append((k, yk, send(part.at[yk, 1 - c], sib.at[k], sibling)))
+        stage_b, stage_a = [], []
+        for k, yk, copy in swaps:
+            copy.wait_recv()
+            part[yk, c] = part[yk, c] + sib[k]
+            if k:
+                stage_b.append(send(part.at[yk, c, :, pl.ds(64, 64), :], b1.at[k - 1], y_of[k]))
+        for k in (1, 2, 3):
+            xk = lax.rem(x + k, X)
+            stage_a.append(send(part.at[:, c, xk, pl.ds(0, 64), :], a1.at[k - 1], x_of[k]))
+        for copy in stage_b:
+            copy.wait_recv()
+        total = part[y, c, :, 64:128, :].astype(F32)
+        for k in range(3):
+            total = total + b1[k].astype(F32)
+        rb[...] = total.astype(BF16)
+        last_b = [
+            send(rb.at[lax.rem(x + k, X)], b2.at[k - 1], x_of[k]) for k in (1, 2, 3)
+        ]
+        for copy in stage_a:
+            copy.wait_recv()
+        total = part[:, c, x, 0:64, :].astype(F32)
+        for k in range(3):
+            total = total + a1[k].astype(F32)
+        ra[...] = total.astype(BF16)
+        last_a = [
+            send(ra.at[lax.rem(y + k, Y)], a2.at[k - 1], y_of[k]) for k in (1, 2, 3)
+        ]
+        for copy in last_a + last_b:
+            copy.wait_recv()
+        half_a = ra[y].astype(F32)
+        half_b = rb[x].astype(F32)
+        for k in range(3):
+            half_a = half_a + a2[k].astype(F32)
+            half_b = half_b + b2[k].astype(F32)
+        return half_a[:, :224], half_b[:, :224]
+
+    heads[z, x] = hv[x]
+    moved = [None] + [
+        send(hv.at[lax.rem(x + k, X)], heads.at[z, x], x_of[k]) for k in (1, 2, 3)
+    ]
+
+    def own_heads(sub):
+        if sub:
+            moved[sub].wait_recv()
+
+    ring_gather(
+        lambda zi, sub: heads.at[zi, lax.rem(x - sub + X, X)], own_heads, lambda zi: None
+    )
+
+    def project(j, _):
+        rows = heads[:, j].reshape(Z * 32, 512)
+        for s, w in enumerate((wo0, wo1, wo2, wo3)):
+            product = jnp.dot(rows, w[...], preferred_element_type=F32).astype(BF16)
+            part_o[j, :, lax.rem(x - s + X, X), :, 0:224] = product.reshape(2, 128, 224)
+        return 0
+
+    lax.fori_loop(0, Y, project, 0)
+
+    halves = reduce_scatter(part_o, sib_o, a1_o, b1_o, ra_o, rb_o, a2_o, b2_o)
+
+    width = pl.ds(pl.multiple_of(x * 256, 256), 256)
+    for h, attended in enumerate(halves):
+        at = pl.ds(64 * h, 64)
+        total = resid[at, :].astype(F32) + attended
+        stream[at, :] = total
+        squares = jnp.sum(total * total, axis=1, keepdims=True)
+        high = squares.astype(BF16).astype(F32)
+        low = squares - high
+        lane = lax.broadcasted_iota(jnp.int32, (64, 32), 1)
+        tail = jnp.where(lane == 0, high, jnp.where(lane == 1, low, 0.0))
+        scaled = jnp.concatenate([total * gain[...].astype(F32), tail], axis=1)
+        normed[y, c, at, width] = scaled.astype(BF16)
+
+    upper, lower = pl.ds(0, 64), pl.ds(64, 64)
+
+    def columns(xk):
+        return pl.ds(pl.multiple_of(xk * 256, 256), 256)
+
+    own_a, own_b = normed.at[y, c, upper, width], normed.at[y, c, lower, width]
+    a_y = [send(own_a, own_a, y_of[k]) for k in (1, 2, 3)]
+    b_x = [send(own_b, own_b, x_of[k]) for k in (1, 2, 3)]
+    a_x = [[send(own_a, own_a, x_of[k]) for k in (1, 2, 3)]]
+    b_y = [[send(own_b, own_b, y_of[k]) for k in (1, 2, 3)]]
+    for k in (1, 2, 3):
+        a_y[k - 1].wait_recv()
+        piece = normed.at[lax.rem(y - k + Y, Y), c, upper, width]
+        a_x.append([send(piece, piece, x_of[j]) for j in (1, 2, 3)])
+        b_x[k - 1].wait_recv()
+        piece = normed.at[y, c, lower, columns(lax.rem(x - k + X, X))]
+        b_y.append([send(piece, piece, y_of[j]) for j in (1, 2, 3)])
+    over = []
+    piece = normed.at[:, c, upper, width]
+    over.append(send(piece, piece, sibling))
+    piece = normed.at[y, c, lower, :]
+    over.append(send(piece, piece, sibling))
+    for k in (1, 2, 3):
+        for group in a_x:
+            group[k - 1].wait_recv()
+        piece = normed.at[:, c, upper, columns(lax.rem(x - k + X, X))]
+        over.append(send(piece, piece, sibling))
+        for group in b_y:
+            group[k - 1].wait_recv()
+        piece = normed.at[lax.rem(y - k + Y, Y), c, lower, :]
+        over.append(send(piece, piece, sibling))
+
+    for load in loads:
+        load.wait()
+    row = lax.broadcasted_iota(jnp.int32, (32, 1280), 0)
+    lane = lax.broadcasted_iota(jnp.int32, (32, 1280), 1)
+    tail = jnp.where((row < 2) & (lane == 576), 1.0, 0.0).astype(BF16)
+    for q in range(X):
+        wgu[256 * q + 224 : 256 * q + 256, :] = tail
+    for copy in over:
+        copy.wait_recv()
+
+    def expand(b):
+        rows = normed[b // 2, lax.rem(b, 2)]
+        terms[b] = jnp.dot(rows, wgu[...], preferred_element_type=F32).astype(BF16)
+
+    def block_at(j):
+        far = 4 - (j + 1) // 2
+        step = jnp.where(lax.rem(j, 2) == 1, far, Z - far)
+        return lax.rem(z + step, Z)
+
+    def expand_range(lo, hi):
+        def body(j, _):
+            expand(block_at(j))
+            return 0
+
+        lax.fori_loop(lo, hi, body, 0)
+
+    def sub_rows(sub):
+        return pl.ds(32 * sub, 32)
+
+    got = {}
+    expand_range(0, 1)
+    far = lax.rem(z + 4, Z)
+    for sub in (0, 1):
+        got["r", 0, sub] = send(
+            terms.at[far, sub_rows(sub)], from_left.at[0, sub_rows(sub)], right
+        )
+        got["l", 0, sub + 2] = send(
+            terms.at[far, sub_rows(sub + 2)], from_right.at[0, sub_rows(sub + 2)], left
+        )
+    expand_range(1, 3)
+    for i in (0, 1):
+        got["r", 1, i + 2] = send(
+            terms.at[lax.rem(z + 3, Z), sub_rows(i + 2)],
+            from_left.at[1, sub_rows(i + 2)],
+            right,
+        )
+        got["l", 1, i] = send(
+            terms.at[lax.rem(z + 5, Z), sub_rows(i)], from_right.at[1, sub_rows(i)], left
+        )
+    expand_range(3, 8)
+
+    def pass_on(step, sub, way):
+        buffer, device = (from_left, right) if way == "r" else (from_right, left)
+        b = lax.rem(z + (4 - step if way == "r" else 4 + step), Z)
+        got[way, step - 1, sub].wait_recv()
+        at = sub_rows(sub)
+        buffer[step - 1, at] = buffer[step - 1, at] + terms[b, at]
+        got[way, step, sub] = send(buffer.at[step - 1, at], buffer.at[step, at], device)
+
+    for i in (0, 1):
+        pass_on(1, i, "r")
+        pass_on(1, i + 2, "l")
+    for step in (2, 3):
+        for i in range(4):
+            pass_on(step, (i + 2) % 4, "r")
+            pass_on(step, i, "l")
+
+    def own_hidden(sub):
+        at = sub_rows(sub)
+        got["r", 3, sub].wait_recv()
+        got["l", 3, sub].wait_recv()
+        total = (
+            terms[z, at].astype(F32) + from_left[3, at].astype(F32) + from_right[3, at].astype(F32)
+        )
+        scale = lax.rsqrt(total[:, 576:577] * (1.0 / D) + EPS)
+        gate, up = total[:, :640] * scale, total[:, 640:] * scale
+        hidden[z, at] = (gate / (1.0 + jnp.exp(-gate)) * up).astype(BF16)
+
+    def contract(b):
+        rows = hidden[b, :, 0:576]
+        for s, w in enumerate((wd0, wd1, wd2, wd3)):
+            product = jnp.dot(rows, w[...], preferred_element_type=F32).astype(BF16)
+            part_d[b // 2, lax.rem(b, 2), lax.rem(x - s + X, X), :, 0:224] = product
+
+    ring_gather(lambda zi, sub: hidden.at[zi, sub_rows(sub)], own_hidden, contract)
+    contract(z)
+
+    halves = reduce_scatter(part_d, sib_d, a1_d, b1_d, ra_d, rb_d, a2_d, b2_d)
+    for h, mlp in enumerate(halves):
+        at = pl.ds(64 * h, 64)
+        out[at, :] = (stream[at, :] + mlp).astype(BF16)
+    for copy in sent:
+        copy.wait_send()
+
+
+COPIES = 176
+
+
+def layer(hv, resid, gain, wgu, wo, wd):
+    vmem = pl.BlockSpec(memory_space=pltpu.VMEM)
+    hbm = pl.BlockSpec(memory_space=pl.ANY)
+    halves = [
+        pltpu.VMEM((3, 4, 64, 256), BF16),
+        pltpu.VMEM((3, 4, 64, 256), BF16),
+        pltpu.VMEM((4, 64, 256), BF16),
+        pltpu.VMEM((4, 64, 256), BF16),
+        pltpu.VMEM((3, 64, 256), BF16),
+        pltpu.VMEM((3, 64, 256), BF16),
+    ]
+    return pl.pallas_call(
+        layer_kernel,
+        out_shape=jax.ShapeDtypeStruct((128, 224), BF16),
+        in_specs=[vmem] * 3 + [hbm] * 4 + [vmem] * 8,
+        out_specs=vmem,
+        scratch_shapes=[
+            pltpu.VMEM((Z, X, 32, 512), BF16),
+            pltpu.VMEM((Y, 2, 128, X * 256), BF16),
+            pltpu.VMEM((X * 256, 1280), BF16),
+            pltpu.VMEM((Y, 2, X, 128, 256), BF16),
+            pltpu.VMEM((Y, 2, X, 128, 256), BF16),
+            pltpu.VMEM((Y, X, 128, 256), BF16),
+            pltpu.VMEM((Y, X, 128, 256), BF16),
+            *halves,
+            *halves,
+            pltpu.VMEM((Z, 128, 1280), BF16),
+            pltpu.VMEM((4, 128, 1280), BF16),
+            pltpu.VMEM((4, 128, 1280), BF16),
+            pltpu.VMEM((Z, 128, 640), BF16),
+            pltpu.VMEM((128, 224), F32),
+            pltpu.SemaphoreType.DMA((COPIES,)),
+            pltpu.SemaphoreType.DMA((COPIES,)),
+            pltpu.SemaphoreType.DMA((4,)),
+        ],
+        compiler_params=pltpu.CompilerParams(
+            collective_id=0, has_side_effects=True, vmem_limit_bytes=52 * 2**20
+        ),
+    )(hv, resid, gain, *wgu, *wo, *wd)
+
+
+def spread(piece, x):
+    got = [piece(x)]
+    for s in range(1, X):
+        pairs = [(i, (i // Z + s) % X * Z + i % Z) for i in range(X * Z)]
+        got.append(lax.ppermute(piece(lax.rem(x + s, X)), "dp", pairs))
+    return got
 
 
 def local(
@@ -94,6 +430,17 @@
     w_up,
     w_down,
 ):
+    x = lax.axis_index("dp") // Z
+
+    def expand_piece(at):
+        gate = lax.dynamic_slice(w_gate, (0, at * 576), (224, 576))
+        up = lax.dynamic_slice(w_up, (0, at * 576), (224, 576))
+        pad = ((0, 0), (0, 64))
+        return jnp.concatenate([jnp.pad(gate, pad), jnp.pad(up, pad)], axis=1)
+
+    wo = spread(lambda at: lax.dynamic_slice(w_o, (at * 512, 0), (512, 224)), x)
+    wgu = spread(expand_piece, x)
+    wd = spread(lambda at: lax.dynamic_slice(w_down, (at * 576, 0), (576, 224)), x)
     head_values = attend_local(
         q_lat,
         q_rope,
@@ -106,37 +453,7 @@
         fresh_len,
         w_uv,
     )
-    attn_terms = jnp.dot(
-        lax.all_gather(head_values, "dp", axis=0, tiled=True),
-        w_o,
-        preferred_element_type=jnp.float32,
-    )
-    gain_f = norm_gain.astype(jnp.float32)
-    attn_part = lax.psum_scatter(
-        attn_terms.astype(jnp.bfloat16), "tensor", scatter_dimension=0, tiled=True
-    ).astype(jnp.float32)
-    stream = resid.astype(jnp.float32) + attn_part
-    squares = lax.psum(jnp.sum(stream * stream, axis=1), "dp")
-    normed = (stream * lax.rsqrt(squares[:, None] / D + epsilon) * gain_f).astype(jnp.bfloat16)
-    all_normed = lax.all_gather(normed, "tensor", axis=0, tiled=True)
-    gate_terms = jnp.dot(all_normed, w_gate, preferred_element_type=jnp.float32)
-    up_terms = jnp.dot(all_normed, w_up, preferred_element_type=jnp.float32)
-    gate_pre, up_pre = (
-        lax.psum_scatter(
-            gate_terms.astype(jnp.bfloat16), "dp", scatter_dimension=0, tiled=True
-        ).astype(jnp.float32),
-        lax.psum_scatter(
-            up_terms.astype(jnp.bfloat16), "dp", scatter_dimension=0, tiled=True
-        ).astype(jnp.float32),
-    )
-    hidden = (jax.nn.silu(gate_pre) * up_pre).astype(jnp.bfloat16)
-    down_terms = jnp.dot(
-        lax.all_gather(hidden, "dp", axis=0, tiled=True), w_down, preferred_element_type=jnp.float32
-    )
-    mlp_part = lax.psum_scatter(
-        down_terms.astype(jnp.bfloat16), "tensor", scatter_dimension=0, tiled=True
-    ).astype(jnp.float32)
-    return (stream + mlp_part).astype(jnp.bfloat16)
+    return layer(head_values, resid, norm_gain.reshape(1, -1), wgu, wo, wd)
 
 
 def solution(mesh):

time: 866 us -> 249 us (0.29)
  waiting for transfers between devices: 663 us -> 17.6 us
  Pallas kernels: 0 us -> 116 us
  blocking collectives: 90 us -> 0 us
  local copies, waits for them, and re-layouts: 22.5 us -> 41.5 us
  between operations: 13.7 us -> 0.27 us
  matrix products: 57.4 us -> 44.8 us
  starting transfers between devices: 0.21 us -> 12.7 us
    reduce_scatter x2 -> x0, waiting for transfers between devices: 434 us -> none  [the longest x1 227 us: local(): lax.psum_scatter(gate_terms.astype(jnp.bfloat16), 'dp', scatter_dimension...]
    all_gather x2 -> x0, waiting for transfers between devices: 168 us -> none  [the longest x1 84.7 us: local(): lax.all_gather(hidden, 'dp', axis=0, tiled=True)]
    pallas_call x0 -> x1, Pallas kernels: none -> 116 us  [layer(): pl.pallas_call(layer_kernel, out_shape=jax.ShapeDtypeStruct((128, 224), B...]
    unnamed x8 -> x0, waiting for transfers between devices: 61.9 us -> none
    psum x1 -> x0, blocking collectives: 61 us -> none  [local(): squares = lax.psum(jnp.sum(stream * stream, axis=1), 'dp')]
    all_gather x1 -> x0, blocking collectives: 29 us -> none  [local(): all_normed = lax.all_gather(normed, 'tensor', axis=0, tiled=True)]
    dot_general x4 -> x0, matrix products: 17.7 us -> none  [the longest x1 4.84 us: local(): gate_terms = jnp.dot(all_normed, w_gate, preferred_element_type=jnp.float32)]
    ppermute x0 -> x9, waiting for transfers between devices: none -> 17.6 us  [spread(): got.append(lax.ppermute(piece(lax.rem(x + s, X)), 'dp', pairs))]
  transfers between devices with their start and end apart: 6 -> 9, of which waited for: 6 -> 2; matrix products, arithmetic and copies ran while one was open for 1% -> 38% of each run, Pallas kernels for 0% -> 0%
where the time goes in v1:
time: 249 us; the launch traced here: 248 us
  Pallas kernels  116 us (47%)
  matrix products  44.8 us (18%)
  local copies, waits for them, and re-layouts  41.5 us (17%)
  waiting for transfers between devices  17.6 us (7%)
  other arithmetic  15.5 us (6%)
  starting transfers between devices  12.7 us (5%)
    pallas_call x1, Pallas kernels, layer(): pl.pallas_call(layer_kernel, out_shape=jax.ShapeDtypeStruct((128, 224), B...  116 us
    dot_general x1, matrix products, attend_local(): jnp.einsum('rhl,kl->rhk', queries, keys_lat, preferred_element_type=jnp.f...  19.2 us
    ppermute x9, waiting for transfers between devices, spread(): got.append(lax.ppermute(piece(lax.rem(x + s, X)), 'dp', pairs))  17.6 us
    unnamed x40, local copies, waits for them, and re-layouts  14.2 us
    dot_general x1, matrix products, attend_local(): jnp.einsum('rhk,kl->rhl', cache_weights, keys_lat, preferred_element_type...  14.1 us
    ppermute x9, starting transfers between devices, spread(): got.append(lax.ppermute(piece(lax.rem(x + s, X)), 'dp', pairs))  12.7 us
    dot_general x1, matrix products, attend_local(): jnp.einsum('rhe,ek->rhk', rope_query, keys_rope, preferred_element_type=j...  9.29 us
    gather x1, local copies, waits for them, and re-layouts, attend_local(): keys_lat = cache_lat[order].reshape(-1, latent_width)  8.94 us
  transfers between devices with their start and end apart: 9, of which 2 were waited for; matrix products, arithmetic and copies ran while one was open for 38% of the time, Pallas kernels for 0%

profile of v1, /device:TPU:1, one launch (start us, length us, event | category | flops | bytes accessed | tf_op | source)
XLA Modules:
  0.0 248.0 jit_solution(8281063959591413302)
XLA Ops:
  0.0 4.0 %constant_dynamic-slice_fusion.7 = (bf16[224,576]{1,0:T(8,128)(2,1)}, bf16[224,576]{1,0:T(8,128)(2,1)S(1)}, bf16[224,576]{1,0:T(8,128)(2,1)}, bf16[224,576]{1,0:...) fusion(bf16[224,2304]{1,0:T(8,128)(2,1)} %param.30, ...), kind=kLoop, calls=%fused_computation.67 | loop fusion | bytes 4128784 | tf_op jit(solution)/shard_map/dynamic_slice | solution.py:437
  4.0 0.9 fusion.17
  4.9 2.0 collective-permute-start
  6.9 0.9 fusion.18
  7.8 2.5 collective-permute-start.1
  10.3 2.2 constant_dynamic-slice_fusion.3
  12.4 0.8 copy.119
  13.2 0.8 copy.120
  14.1 2.3 collective-permute-start.4
  16.4 2.7 %constant_dynamic-slice_fusion.15 = (bf16[576,224]{0,1:T(8,128)(2,1)}, bf16[576,224]{0,1:T(8,128)(2,1)}, bf16[576,224]{0,1:T(8,128)(2,1)S(1)}, bf16[576,224]{0,1:T(8,128)(2,1)}) fusion(bf16[2304,224]{0,1:T(8,128)(2,1)} %param.31, s32[]{:T(128)S(6)} %select_n.95, s32[]{:T(128)S(6)} %select_n.94, s32[]{:T(128)S(6)} %select_n.93, s32[]{:T(128)S(6)} %select_n.92), kind=kLoop, calls=%fused_computation.75 | loop fusion | bytes 2064400 | tf_op jit(solution)/shard_map/dynamic_slice | solution.py:443
  19.1 0.9 copy.123
  20.0 0.9 collective-permute-start.6
  20.9 0.1 reshape_squeeze.3
  21.0 0.0 copy-start.13
  21.0 0.0 copy-start.11
  21.0 8.9 %gather_fusion = bf16[64,128,512]{2,1,0:T(8,128)(2,1)} fusion(bf16[64,128,512]{2,1,0:T(8,128)(2,1)} %param.20, s32[1024]{0:T(1024)S(1)} %pad_clamp_fusion), kind=kCustom, calls=%fused_computation | custom fusion | bytes 16777472 | tf_op jit(solution)/shard_map/gather | solution.py:37
  30.0 2.9 %gather_fusion.1 = bf16[64,64,128]{2,1,0:T(8,128)(2,1)} fusion(bf16[64,64,128]{2,1,0:T(8,128)(2,1)} %param.21, s32[1024]{0:T(1024)S(1)} %pad_clamp_fusion), kind=kCustom, calls=%fused_computation.1 | custom fusion | bytes 2097408 | tf_op jit(solution)/shard_map/gather | solution.py:38
  32.9 2.9 %copy.95 = bf16[64,64,128]{2,1,0:T(8,128)(2,1)} copy(bf16[64,64,128]{2,0,1:T(8,128)(2,1)} %bitcast.45) | data formatting | bytes 2097152 | tf_op jit(solution)/shard_map/transpose | solution.py:38
  35.7 2.3 reshape.214
  38.1 0.1 reshape.194
  38.2 0.2 reduce-window.4
  38.5 0.2 fusion.27
  38.6 0.1 fusion.40
  38.7 0.9 compare_and_fusion
  39.6 1.2 copy.127
  40.9 0.0 copy-start.8
  40.9 0.0 copy-start.10
  40.9 9.3 %fusion.25 = f32[8192,32,16]{0,1,2:T(8,128)} fusion(bf16[64,8192,1]{1,0,2:T(8,128)(2,1)} %reshape.214, bf16[32,16,64]{2,1,0:T(8,128)(2,1)S(1)} %reshape.194), kind=kOutput, calls=%fused_computation.37 | convolution fusion | flops 536870912 | bytes 17891328 | tf_op jit(solution)/shard_map/rhe,ek->rhk/dot_general | solution.py:61
  50.2 0.3 fusion.38
  50.4 0.3 fusion.44
  50.7 0.1 copy.99
  50.8 19.2 %fusion.43 = (f32[32,16]{0,1:T(8,128)S(1)}, f32[32,16,8192]{2,0,1:T(8,128)}) fusion(f32[8192,32,16]{0,1,2:T(8,128)} %fusion.25, bf16[8192,512,1]{1,0,2:T(8,128)(2,1)} %bitcast.43, bf16[4,16,8,512]{3,2,1,0:T(8,128)(2,1)} %bitcast.48, pred[32,8192]{1,0:T(8,128)(4,1)} %compare_and_fusion), kind=kOutput, calls=%fused_computation.79 | convolution fusion | flops 4311744000 | bytes 42731520 | tf_op jit(solution)/shard_map/rhl,kl->rhk/dot_general | solution.py:60
  70.0 0.1 copy.100
  70.1 8.1 %fusion = f32[32,16]{0,1:T(8,128)S(1)} fusion(f32[32,16,8192]{2,0,1:T(8,128)} %get-tuple-element.22, f32[32,16]{0,1:T(8,128)S(1)} %max.7), kind=kLoop, calls=%fused_computation.5 | loop fusion | flops 8388096 | bytes 16781312 | tf_op jit(solution)/shard_map/reduce_sum | solution.py:72
  78.2 0.3 fusion.22
  78.4 0.1 copy.101
  78.5 14.1 %fusion.1 = f32[32,16,512]{2,0,1:T(8,128)} fusion(bf16[8192,512,1]{1,0,2:T(8,128)(2,1)} %bitcast.44, f32[32,16,8192]{2,0,1:T(8,128)} %get-tuple-element.22, f32[32,16]{0,1:T(8,128)S(1)} %add.115, f32[32,16]{0,1:T(8,128)S(1)} %max.7), kind=kOutput, calls=%fused_computation.6 | convolution fusion | flops 4307550208 | bytes 26218496 | tf_op jit(solution)/shard_map/rhk,kl->rhl/dot_general | solution.py:76
  92.6 0.9 fusion.19
  93.5 0.1 copy.102
  93.6 1.8 copy.121
  95.3 0.0 collective-permute-done.3.wo1
  95.3 1.8 collective-permute-start.2
  97.1 0.0 collective-permute-done.4.wo2
  97.1 0.1 collective-permute-start.5
  97.2 1.2 divide_convert_fusion.2
  98.4 1.8 copy.124
  100.2 1.8 copy.125
  102.1 11.5 %collective-permute-done.5.wo3 = bf16[512,224]{1,0:T(8,128)(2,1)S(1)} collective-permute-done((bf16[512,224]{1,0:T(8,128)(2,1)}, bf16[512,224]{1,0:T(8,128)(2,1)S(1)}, u32[]{:S(2)}, u32[]{:S(2)}) %collective-permute-start.5) | collective-permute-done | bytes 229408 | tf_op jit(solution)/shard_map/ppermute | solution.py:411
  113.5 1.6 collective-permute-start.7
  115.2 1.5 collective-permute-start.8
  116.6 1.8 fusion.15
  118.4 0.1 copy.104
  118.5 0.1 reshape.195
  118.6 0.9 copy.114.resid
  119.5 1.1 copy.118.wo0
  120.6 1.1 copy.122.wd0
  121.7 1.9 fusion.16.wgu0
  123.7 6.1 %collective-permute-done.8.wd3 = bf16[576,224]{1,0:T(8,128)(2,1)} collective-permute-done((bf16[576,224]{1,0:T(8,128)(2,1)}, bf16[576,224]{1,0:T(8,128)(2,1)}, u32[]{:S(2)}, u32[]{:S(2)}) %collective-permute-start.8) | collective-permute-done | bytes 258080 | tf_op jit(solution)/shard_map/ppermute | solution.py:411
  129.8 0.0 collective-permute-done.wgu1
  129.8 0.0 collective-permute-done.1.wgu2
  129.8 0.9 copy-done.2
  130.8 0.9 copy-done.4
  131.7 115.6 %shard_map.154 = bf16[128,224]{1,0:T(8,128)(2,1)S(1)} custom-call(bf16[4,32,512]{2,1,0:T(8,128)(2,1)S(1)} %bitcast.42, bf16[128,224]{1,0:T(8,128)(2,1)S(1)} %copy.114.resid, bf16[1,224]{1,0:T(2,128)(2,1)S(1)} %reshape.196.gain, bf16[224,1280]{1,0:T(8,128)(2,1)} %fusion.16.wgu0, bf16[224,1280]{1,0:T(8,128)(2,1)} %collective-permute-done.wgu1, ...), custom_call_target="tpu_custom_call" | custom-call | tf_op jit(solution)/shard_map/pallas_call | solution.py:377
  247.3 0.7 copy.115
  (37 shorter events, 0.2 us)
Async XLA Ops:
  0.0 116.6 %copy-start = (bf16[16,512,128]{2,1,0:T(8,128)(2,1)S(1)}, bf16[16,512,128]{2,1,0:T(8,128)(2,1)}, u32[]{:S(2)}) copy-start(bf16[16,512,128]{2,1,0:T(8,128)(2,1)} %param.25) | copy-start | bytes 6291460
  0.0 20.9 %copy-start.12 = (s32[1,2,32]{2,1,0:T(2,128)S(1)}, s32[1,2,32]{2,1,0:T(2,128)}, u32[]{:S(2)}) copy-start(s32[1,2,32]{2,1,0:T(2,128)} %param.22) | copy-start | bytes 772
  4.9 124.9 %collective-permute-start = (bf16[224,1280]{1,0:T(8,128)(2,1)}, bf16[224,1280]{1,0:T(8,128)(2,1)}, u32[]{:S(2)}, u32[]{:S(2)}) collective-permute-start(bf16[224,1280]{1,0:T(8,128)(2,1)} %fusion.17), channel_id=1, source_target_pairs={{0,64},{8,72},{16,80},{24,88},{32,96},{40,104},{48,112},{56,120},{... | collective-permute-start | bytes 1720328 | tf_op jit(solution)/shard_map/ppermute | solution.py:411
  7.8 122.0 %collective-permute-start.1 = (bf16[224,1280]{1,0:T(8,128)(2,1)}, bf16[224,1280]{1,0:T(8,128)(2,1)}, u32[]{:S(2)}, u32[]{:S(2)}) collective-permute-start(bf16[224,1280]{1,0:T(8,128)(2,1)} %fusion.18), channel_id=1, source_target_pairs={{0,128},{8,136},{16,144},{24,152},{32,160},{40,168},{48,176},{56,1... | collective-permute-start | bytes 1720328 | tf_op jit(solution)/shard_map/ppermute | solution.py:411
  13.2 82.1 %collective-permute-start.3 = (bf16[512,224]{1,0:T(8,128)(2,1)}, bf16[512,224]{1,0:T(8,128)(2,1)S(1)}, u32[]{:S(2)}, u32[]{:S(2)}) collective-permute-start(bf16[512,224]{1,0:T(8,128)(2,1)} %copy.119), channel_id=1, source_target_pairs={{0,64},{8,72},{16,80},{24,88},{32,96},{40,104},{48,112},{56,120},{... | collective-permute-start | bytes 688136 | tf_op jit(solution)/shard_map/ppermute | solution.py:411
  14.1 83.1 %collective-permute-start.4 = (bf16[512,224]{1,0:T(8,128)(2,1)}, bf16[512,224]{1,0:T(8,128)(2,1)S(1)}, u32[]{:S(2)}, u32[]{:S(2)}) collective-permute-start(bf16[512,224]{1,0:T(8,128)(2,1)} %copy.120), channel_id=1, source_target_pairs={{0,128},{8,136},{16,144},{24,152},{32,160},{40,168},{48,176},{56,1... | collective-permute-start | bytes 688136 | tf_op jit(solution)/shard_map/ppermute | solution.py:411
  20.0 95.2 %collective-permute-start.6 = (bf16[576,224]{1,0:T(8,128)(2,1)}, bf16[576,224]{1,0:T(8,128)(2,1)S(1)}, u32[]{:S(2)}, u32[]{:S(2)}) collective-permute-start(bf16[576,224]{1,0:T(8,128)(2,1)} %copy.123), channel_id=1, source_target_pairs={{0,64},{8,72},{16,80},{24,88},{32,96},{40,104},{48,112},{56,120},{... | collective-permute-start | bytes 774152 | tf_op jit(solution)/shard_map/ppermute | solution.py:411
  21.0 17.1 %copy-start.9 = (bf16[32,1024]{1,0:T(8,128)(2,1)S(1)}, bf16[32,1024]{1,0:T(8,128)(2,1)}, u32[]{:S(2)}) copy-start(bf16[32,1024]{1,0:T(8,128)(2,1)} %param.17) | copy-start | bytes 196612
  21.0 17.2 %copy-start.13 = (s32[1,2]{1,0:T(1,128)S(1)}, s32[1,2]{1,0:T(1,128)}, u32[]{:S(2)}) copy-start(s32[1,2]{1,0:T(1,128)} %param.24) | copy-start | bytes 28
  21.0 17.4 %copy-start.11 = (s32[1,2]{1,0:T(1,128)S(1)}, s32[1,2]{1,0:T(1,128)}, u32[]{:S(2)}) copy-start(s32[1,2]{1,0:T(1,128)} %param.23) | copy-start | bytes 28
  40.9 9.3 %copy-start.8 = (bf16[32,512]{1,0:T(8,128)(2,1)S(1)}, bf16[32,512]{1,0:T(8,128)(2,1)}, u32[]{:S(2)}) copy-start(bf16[32,512]{1,0:T(8,128)(2,1)} %param.18) | copy-start | bytes 98308
  40.9 9.6 %copy-start.10 = (bf16[32,64]{1,0:T(8,128)(2,1)S(1)}, bf16[32,64]{1,0:T(8,128)(2,1)}, u32[]{:S(2)}) copy-start(bf16[32,64]{1,0:T(8,128)(2,1)} %param.19) | copy-start | bytes 12292
  50.7 27.4 %copy-start.5 = (f32[32,16,32]{2,1,0:T(8,128)}, f32[32,16,32]{2,1,0:T(8,128)S(1)}, u32[]{:S(2)}) copy-start(f32[32,16,32]{2,1,0:T(8,128)S(1)} %get-tuple-element.24) | copy-start | bytes 196612
  78.5 14.1 %copy-start.6 = (bf16[224,576]{1,0:T(8,128)(2,1)S(1)}, bf16[224,576]{1,0:T(8,128)(2,1)}, u32[]{:S(2)}) copy-start(bf16[224,576]{1,0:T(8,128)(2,1)} %get-tuple-element.13) | copy-start | bytes 774148
  78.5 14.1 %copy-start.7 = (bf16[224,576]{1,0:T(8,128)(2,1)S(1)}, bf16[224,576]{1,0:T(8,128)(2,1)}, u32[]{:S(2)}) copy-start(bf16[224,576]{1,0:T(8,128)(2,1)} %get-tuple-element.28) | copy-start | bytes 774148
  78.5 41.0 %copy-start.14 = (bf16[224]{0:T(256)(128)(2,1)S(1)}, bf16[224]{0:T(256)(128)(2,1)}, u32[]{:S(2)}) copy-start(bf16[224]{0:T(256)(128)(2,1)} %param.28) | copy-start | bytes 1348
  95.3 34.5 %collective-permute-start.2 = (bf16[224,1280]{1,0:T(8,128)(2,1)}, bf16[224,1280]{1,0:T(8,128)(2,1)}, u32[]{:S(2)}, u32[]{:S(2)}) collective-permute-start(bf16[224,1280]{1,0:T(8,128)(2,1)} %fusion.19), channel_id=1, source_target_pairs={{0,192},{8,200},{16,208},{24,216},{32,224},{40,232},{48,240},{56,2... | collective-permute-start | bytes 1720328 | tf_op jit(solution)/shard_map/ppermute | solution.py:411
  97.1 23.5 %copy-start.1 = (bf16[512,224]{1,0:T(8,128)(2,1)}, bf16[512,224]{1,0:T(8,128)(2,1)S(1)}, u32[]{:S(2)}) copy-start(bf16[512,224]{1,0:T(8,128)(2,1)S(1)} %collective-permute-done.4.wo2) | copy-start | bytes 688132
  97.1 16.4 %collective-permute-start.5 = (bf16[512,224]{1,0:T(8,128)(2,1)}, bf16[512,224]{1,0:T(8,128)(2,1)S(1)}, u32[]{:S(2)}, u32[]{:S(2)}) collective-permute-start(bf16[512,224]{1,0:T(8,128)(2,1)} %copy.121), channel_id=1, source_target_pairs={{0,192},{8,200},{16,208},{24,216},{32,224},{40,232},{48,240},{56,2... | collective-permute-start | bytes 688136 | tf_op jit(solution)/shard_map/ppermute | solution.py:411
  113.5 6.0 %copy-start.3 = (bf16[512,224]{1,0:T(8,128)(2,1)}, bf16[512,224]{1,0:T(8,128)(2,1)S(1)}, u32[]{:S(2)}) copy-start(bf16[512,224]{1,0:T(8,128)(2,1)S(1)} %collective-permute-done.5.wo3) | copy-start | bytes 688132
  113.5 10.1 %collective-permute-start.7 = (bf16[576,224]{1,0:T(8,128)(2,1)}, bf16[576,224]{1,0:T(8,128)(2,1)}, u32[]{:S(2)}, u32[]{:S(2)}) collective-permute-start(bf16[576,224]{1,0:T(8,128)(2,1)} %copy.124), channel_id=1, source_target_pairs={{0,128},{8,136},{16,144},{24,152},{32,160},{40,168},{48,176},{56,1... | collective-permute-start | bytes 774152 | tf_op jit(solution)/shard_map/ppermute | solution.py:411
  115.2 14.6 %collective-permute-start.8 = (bf16[576,224]{1,0:T(8,128)(2,1)}, bf16[576,224]{1,0:T(8,128)(2,1)}, u32[]{:S(2)}, u32[]{:S(2)}) collective-permute-start(bf16[576,224]{1,0:T(8,128)(2,1)} %copy.125), channel_id=1, source_target_pairs={{0,192},{8,200},{16,208},{24,216},{32,224},{40,232},{48,240},{56,2... | collective-permute-start | bytes 774152 | tf_op jit(solution)/shard_map/ppermute | solution.py:411
  129.8 1.0 copy-start.2
  130.8 0.9 copy-start.4

commit v2 on v1

--- a/solution.py
+++ b/solution.py
@@ -15,78 +15,163 @@
 MESH = pl.DeviceIdType.MESH
 F32 = jnp.float32
 BF16 = jnp.bfloat16
-
-
-def attend_local(
-    q_lat,
-    q_rope,
-    fresh_lat,
-    fresh_rope,
-    cache_lat,
-    cache_rope,
-    page_table,
-    hit_len,
-    fresh_len,
-    w_uv,
+CHUNK = 512
+AHEAD = 3
+LOW = -1e30
+QUERIES = 384
+
+
+def attend_kernel(
+    table, hit, count, q_lat, q_rope, fresh_lat, fresh_rope, cache_lat, cache_rope, w_uv,
+    out,
+    q_all, r_all, shuffle, keys, ropes, peak, mass, acc, w_uv_here, sem, uv_sem,
 ):
-    heads, latent_width, value_width = w_uv.shape
-    rows_here = fresh_lat.shape[0]
-    queries = q_lat.reshape(rows_here, heads, latent_width)
-    rope_query = q_rope.reshape(rows_here, heads, fresh_rope.shape[1])
-    order = page_table[0].reshape(-1)
-    keys_lat = cache_lat[order].reshape(-1, latent_width)
-    keys_rope = jnp.transpose(cache_rope[order], (1, 0, 2)).reshape(cache_rope.shape[1], -1)
-    counts = fresh_len[0]
-    hit = hit_len[0]
-    row_ids = jnp.arange(rows_here, dtype=jnp.int32)
-    bounds = jnp.cumsum(counts)[:-1]
-    row_request = jnp.sum((row_ids[:, None] >= bounds[None, :]).astype(jnp.int32), axis=1)
-    key_ids = jnp.arange(keys_lat.shape[0], dtype=jnp.int32)
-    span_len = keys_lat.shape[0] // counts.shape[0]
-    key_request = key_ids // span_len
-    key_place = key_ids % span_len
-    request_ids = jnp.arange(counts.shape[0], dtype=jnp.int32)
-    limits = jnp.sum(
-        jnp.where(key_request[:, None] == request_ids[None, :], hit[None, :], 0), axis=1
-    )
-    cache_mask = (row_request[:, None] == key_request[None, :]) & (
-        key_place[None, :] < limits[None, :]
-    )
-    fresh_mask = (row_request[:, None] == row_request[None, :]) & (
-        row_ids[None, :] <= row_ids[:, None]
-    )
-    factor = (VDIM + ROPE) ** (-0.5)
-    cache_scores = factor * (
-        jnp.einsum("rhl,kl->rhk", queries, keys_lat, preferred_element_type=jnp.float32)
-        + jnp.einsum("rhe,ek->rhk", rope_query, keys_rope, preferred_element_type=jnp.float32)
-    )
-    fresh_scores = factor * (
-        jnp.einsum("rhl,jl->rhj", queries, fresh_lat, preferred_element_type=jnp.float32)
-        + jnp.einsum("rhe,je->rhj", rope_query, fresh_rope, preferred_element_type=jnp.float32)
-    )
-    cache_scores = jnp.where(cache_mask[:, None, :], cache_scores, -jnp.inf)
-    fresh_scores = jnp.where(fresh_mask[:, None, :], fresh_scores, -jnp.inf)
-    peak = jnp.maximum(jnp.max(cache_scores, axis=2), jnp.max(fresh_scores, axis=2))
-    cache_exp = jnp.exp(cache_scores - peak[..., None])
-    fresh_exp = jnp.exp(fresh_scores - peak[..., None])
-    denominator = jnp.sum(cache_exp, axis=2) + jnp.sum(fresh_exp, axis=2)
-    cache_weights = (cache_exp / denominator[..., None]).astype(jnp.bfloat16)
-    fresh_weights = (fresh_exp / denominator[..., None]).astype(jnp.bfloat16)
-    latent_out = (
-        jnp.einsum("rhk,kl->rhl", cache_weights, keys_lat, preferred_element_type=jnp.float32)
-        + jnp.einsum("rhj,jl->rhl", fresh_weights, fresh_lat, preferred_element_type=jnp.float32)
-    ).astype(jnp.bfloat16)
-    values = jnp.einsum(
-        "rhl,hlv->rhv", latent_out, w_uv, preferred_element_type=jnp.float32
-    ).astype(jnp.bfloat16)
-    return jnp.transpose(values.reshape(rows_here, X, -1), (1, 0, 2))
+    pages = CHUNK // 128
+    chunks0 = (hit[0, 0] + CHUNK - 1) // CHUNK
+    chunks1 = (hit[0, 1] + CHUNK - 1) // CHUNK
+    chunks = chunks0 + chunks1
+
+    def place(i):
+        r = (i >= chunks0).astype(jnp.int32)
+        return r, i - r * chunks0
+
+    def page_copies(i, j):
+        r, k = place(i)
+        page = table[0, r, k * pages + j]
+        return (
+            pltpu.make_async_copy(
+                cache_lat.at[page], keys.at[i, pl.ds(128 * j, 128), :], sem.at[0, i, j]
+            ),
+            pltpu.make_async_copy(
+                cache_rope.at[page], ropes.at[i, :, pl.ds(128 * j, 128)], sem.at[1, i, j]
+            ),
+        )
+
+    def fetch(i):
+        @pl.when(i < chunks)
+        def _():
+            for j in range(pages):
+                for copy in page_copies(i, j):
+                    copy.start()
+
+    for i in range(AHEAD):
+        fetch(jnp.int32(i))
+    uv_copy = pltpu.make_async_copy(w_uv, w_uv_here, uv_sem)
+    uv_copy.start()
+
+    for h in range(16):
+        for j in range(4):
+            shuffle[j, pl.ds(h, 32, stride=16), :] = q_lat[
+                :, 512 * h + 128 * j : 512 * h + 128 * (j + 1)
+            ].astype(F32)
+    for j in range(4):
+        q_all[:, 128 * j : 128 * (j + 1)] = shuffle[j].astype(BF16)
+    for h in range(0, 16, 2):
+        pair = q_rope[:, 64 * h : 64 * h + 128].astype(F32)
+        shuffle[0, pl.ds(h, 32, stride=16), :] = pair
+        shuffle[0, pl.ds(h + 1, 32, stride=16), :] = jnp.concatenate(
+            [pair[:, 64:], pair[:, :64]], axis=1
+        )
+    r_all[...] = shuffle[0, :, 0:64].astype(BF16)
+
+    scale = (VDIM + ROPE) ** -0.5 * 1.4426950408889634
+    n0 = count[0, 0]
+
+    def nt(a, b):
+        return lax.dot_general(a, b, (((1,), (1,)), ((), ())), preferred_element_type=F32)
+
+    scores = (nt(q_all[...], fresh_lat[...]) + nt(r_all[...], fresh_rope[...])) * scale
+    row = lax.broadcasted_iota(jnp.int32, (512, 32), 0) // 16
+    key = lax.broadcasted_iota(jnp.int32, (512, 32), 1)
+    valid = (key <= row) & ((key >= n0) | (row < n0))
+    scores = jnp.where(valid, scores, LOW)
+    top = jnp.max(scores, axis=1, keepdims=True)
+    weight = jnp.exp2(scores - top)
+    peak[...] = top
+    mass[...] = jnp.sum(weight, axis=1, keepdims=True)
+    product = jnp.dot(weight.astype(BF16), fresh_lat[...], preferred_element_type=F32)
+    for j in range(4):
+        acc[j] = product[:, 128 * j : 128 * (j + 1)]
+
+    def body(i, _):
+        fetch(i + AHEAD)
+        r, k = place(i)
+        start = pl.multiple_of(r * 128, 128)
+        at = pl.ds(start, QUERIES)
+        for j in range(pages):
+            for copy in page_copies(i, j):
+                copy.wait()
+        block = keys[i]
+        scores = nt(q_all[at, :], block) + jnp.dot(
+            r_all[at, :], ropes[i], preferred_element_type=F32
+        )
+        position = k * CHUNK + lax.broadcasted_iota(jnp.int32, (1, CHUNK), 1)
+        query = start + lax.broadcasted_iota(jnp.int32, (QUERIES, 1), 0)
+        first = r * n0 * 16
+        last = jnp.where(r == 0, n0 * 16, 512)
+        column_bias = jnp.where(position < hit[0, r], 0.0, LOW)
+        row_bias = jnp.where((query >= first) & (query < last), 0.0, LOW)
+        scores = scores * scale + column_bias + row_bias
+        before = peak[at, :]
+        top = jnp.maximum(before, jnp.max(scores, axis=1, keepdims=True))
+        shrink = jnp.exp2(before - top)
+        weight = jnp.exp2(scores - top)
+        peak[at, :] = top
+        mass[at, :] = mass[at, :] * shrink + jnp.sum(weight, axis=1, keepdims=True)
+        product = jnp.dot(weight.astype(BF16), block, preferred_element_type=F32)
+        for j in range(4):
+            acc[j, at, :] = acc[j, at, :] * shrink + product[:, 128 * j : 128 * (j + 1)]
+        return 0
+
+    lax.fori_loop(0, chunks, body, 0)
+
+    uv_copy.wait()
+    inverse = 1.0 / mass[...]
+    for j in range(4):
+        acc[j] = acc[j] * inverse
+    for h in range(16):
+        rows = jnp.concatenate(
+            [acc[j, pl.ds(h, 32, stride=16), :] for j in range(4)], axis=1
+        ).astype(BF16)
+        values = jnp.dot(rows, w_uv_here[h], preferred_element_type=F32).astype(BF16)
+        out[h // 4, :, 128 * (h % 4) : 128 * (h % 4 + 1)] = values
+
+
+def attend(q_lat, q_rope, fresh_lat, fresh_rope, cache_lat, cache_rope, page_table, hit_len, fresh_len, w_uv):
+    vmem = pl.BlockSpec(memory_space=pltpu.VMEM)
+    smem = pl.BlockSpec(memory_space=pltpu.SMEM)
+    hbm = pl.BlockSpec(memory_space=pl.ANY)
+    most = 8192 // CHUNK
+    return pl.pallas_call(
+        attend_kernel,
+        out_shape=jax.ShapeDtypeStruct((4, 32, 512), BF16),
+        in_specs=[smem] * 3 + [vmem] * 4 + [hbm] * 3,
+        out_specs=vmem,
+        scratch_shapes=[
+            pltpu.VMEM((512, 512), BF16),
+            pltpu.VMEM((512, 64), BF16),
+            pltpu.VMEM((4, 512, 128), F32),
+            pltpu.VMEM((most, CHUNK, 512), BF16),
+            pltpu.VMEM((most, 64, CHUNK), BF16),
+            pltpu.VMEM((512, 1), F32),
+            pltpu.VMEM((512, 1), F32),
+            pltpu.VMEM((4, 512, 128), F32),
+            pltpu.VMEM((16, 512, 128), BF16),
+            pltpu.SemaphoreType.DMA((2, most, CHUNK // 128)),
+            pltpu.SemaphoreType.DMA,
+        ],
+        compiler_params=pltpu.CompilerParams(vmem_limit_bytes=61 * 2**20),
+        cost_estimate=pl.CostEstimate(
+            flops=20 * 10**9, bytes_accessed=12 * 2**20, transcendentals=2**22
+        ),
+    )(page_table, hit_len, fresh_len, q_lat, q_rope, fresh_lat, fresh_rope, cache_lat, cache_rope, w_uv)
 
 
 def layer_kernel(
     hv, resid, gain,
-    wgu0, wgu1, wgu2, wgu3, wo0, wo1, wo2, wo3, wd0, wd1, wd2, wd3,
+    w_gate, w_up, wgu1, wgu2, wgu3, w_o, w_down,
     out,
-    heads, normed, wgu, part_o, part_d, sib_o, sib_d,
+    heads, normed, wgu, wo, wd, part_o, part_d, sib_o, sib_d,
     a1_o, b1_o, ra_o, rb_o, a2_o, b2_o,
     a1_d, b1_d, ra_d, rb_d, a2_d, b2_d,
     terms, from_left, from_right, hidden, stream,
@@ -106,12 +191,32 @@
     y_of = [near(dy=k) for k in range(Y)]
     right, left, sibling = near(dz=1), near(dz=Z - 1), near(dc=1)
 
-    loads = []
-    for s, block in enumerate((wgu0, wgu1, wgu2, wgu3)):
-        row = pl.multiple_of(lax.rem(x - s + X, X) * 256, 256)
-        load = pltpu.make_async_copy(block, wgu.at[pl.ds(row, 224), :], wsem.at[s])
+    def window(xk):
+        return pl.ds(pl.multiple_of((9 * xk) // 2 * 128, 128), 640)
+
+    def block_rows(xk):
+        return pl.ds(pl.multiple_of(xk * 256, 256), 224)
+
+    loads = [
+        pltpu.make_async_copy(
+            w_o.at[:, pl.ds(pl.multiple_of(x * 512, 512), 512)], wo.at[0], wsem.at[0]
+        ),
+        pltpu.make_async_copy(
+            w_gate.at[:, window(x)], wgu.at[block_rows(x), pl.ds(0, 640)], wsem.at[1]
+        ),
+        pltpu.make_async_copy(
+            w_up.at[:, window(x)], wgu.at[block_rows(x), pl.ds(640, 640)], wsem.at[2]
+        ),
+        pltpu.make_async_copy(w_down.at[:, window(x)], wd.at[0], wsem.at[3]),
+    ]
+    for s, block in enumerate((wgu1, wgu2, wgu3)):
+        loads.append(
+            pltpu.make_async_copy(
+                block, wgu.at[block_rows(lax.rem(x - s - 1 + X, X)), :], wsem.at[4 + s]
+            )
+        )
+    for load in loads:
         load.start()
-        loads.append(load)
 
     barrier = pltpu.get_barrier_semaphore()
     partners = x_of[1:] + y_of[1:] + [right, left, sibling]
@@ -201,6 +306,15 @@
         send(hv.at[lax.rem(x + k, X)], heads.at[z, x], x_of[k]) for k in (1, 2, 3)
     ]
 
+    wo_moves = [
+        send(
+            w_o.at[:, pl.ds(pl.multiple_of(lax.rem(x + k, X) * 512, 512), 512)],
+            wo.at[k],
+            x_of[k],
+        )
+        for k in (1, 2, 3)
+    ]
+
     def own_heads(sub):
         if sub:
             moved[sub].wait_recv()
@@ -209,10 +323,17 @@
         lambda zi, sub: heads.at[zi, lax.rem(x - sub + X, X)], own_heads, lambda zi: None
     )
 
+    loads[0].wait()
+    for copy in wo_moves:
+        copy.wait_recv()
+
+    def nt(a, b):
+        return lax.dot_general(a, b, (((1,), (1,)), ((), ())), preferred_element_type=F32)
+
     def project(j, _):
         rows = heads[:, j].reshape(Z * 32, 512)
-        for s, w in enumerate((wo0, wo1, wo2, wo3)):
-            product = jnp.dot(rows, w[...], preferred_element_type=F32).astype(BF16)
+        for s in range(X):
+            product = nt(rows, wo[s]).astype(BF16)
             part_o[j, :, lax.rem(x - s + X, X), :, 0:224] = product.reshape(2, 128, 224)
         return 0
 
@@ -265,11 +386,18 @@
         piece = normed.at[lax.rem(y - k + Y, Y), c, lower, :]
         over.append(send(piece, piece, sibling))
 
-    for load in loads:
+    for load in loads[1:]:
         load.wait()
+    odd = lax.rem(x, 2)
+    edge = pl.multiple_of((1 - odd) * 512, 128)
+    lane = lax.broadcasted_iota(jnp.int32, (1, 128), 1)
+    mine = (lane >= 64 * odd) & (lane < 64 + 64 * odd)
+    for start in (edge, 640 + edge):
+        tile = pl.ds(pl.multiple_of(start, 128), 128)
+        wgu[:, tile] = jnp.where(mine, wgu[:, tile].astype(F32), 0.0).astype(BF16)
     row = lax.broadcasted_iota(jnp.int32, (32, 1280), 0)
     lane = lax.broadcasted_iota(jnp.int32, (32, 1280), 1)
-    tail = jnp.where((row < 2) & (lane == 576), 1.0, 0.0).astype(BF16)
+    tail = jnp.where((row < 2) & (lane == 576 * (1 - odd)), 1.0, 0.0).astype(BF16)
     for q in range(X):
         wgu[256 * q + 224 : 256 * q + 256, :] = tail
     for copy in over:
@@ -314,6 +442,9 @@
         got["l", 1, i] = send(
             terms.at[lax.rem(z + 5, Z), sub_rows(i)], from_right.at[1, sub_rows(i)], left
         )
+    wd_moves = [
+        send(w_down.at[:, window(lax.rem(x + k, X))], wd.at[k], x_of[k]) for k in (1, 2, 3)
+    ]
     expand_range(3, 8)
 
     def pass_on(step, sub, way):
@@ -339,16 +470,19 @@
         total = (
             terms[z, at].astype(F32) + from_left[3, at].astype(F32) + from_right[3, at].astype(F32)
         )
-        scale = lax.rsqrt(total[:, 576:577] * (1.0 / D) + EPS)
+        squares = jnp.where(odd == 1, total[:, 0:1], total[:, 576:577])
+        scale = lax.rsqrt(squares * (1.0 / D) + EPS)
         gate, up = total[:, :640] * scale, total[:, 640:] * scale
         hidden[z, at] = (gate / (1.0 + jnp.exp(-gate)) * up).astype(BF16)
 
     def contract(b):
-        rows = hidden[b, :, 0:576]
-        for s, w in enumerate((wd0, wd1, wd2, wd3)):
-            product = jnp.dot(rows, w[...], preferred_element_type=F32).astype(BF16)
+        rows = hidden[b]
+        for s in range(X):
+            product = nt(rows, wd[s]).astype(BF16)
             part_d[b // 2, lax.rem(b, 2), lax.rem(x - s + X, X), :, 0:224] = product
 
+    for copy in wd_moves:
+        copy.wait_recv()
     ring_gather(lambda zi, sub: hidden.at[zi, sub_rows(sub)], own_hidden, contract)
     contract(z)
 
@@ -363,7 +497,7 @@
 COPIES = 176
 
 
-def layer(hv, resid, gain, wgu, wo, wd):
+def layer(hv, resid, gain, w_gate, w_up, wgu, w_o, w_down):
     vmem = pl.BlockSpec(memory_space=pltpu.VMEM)
     hbm = pl.BlockSpec(memory_space=pl.ANY)
     halves = [
@@ -377,12 +511,14 @@
     return pl.pallas_call(
         layer_kernel,
         out_shape=jax.ShapeDtypeStruct((128, 224), BF16),
-        in_specs=[vmem] * 3 + [hbm] * 4 + [vmem] * 8,
+        in_specs=[vmem] * 3 + [hbm] * 7,
         out_specs=vmem,
         scratch_shapes=[
             pltpu.VMEM((Z, X, 32, 512), BF16),
             pltpu.VMEM((Y, 2, 128, X * 256), BF16),
             pltpu.VMEM((X * 256, 1280), BF16),
+            pltpu.VMEM((X, 224, 512), BF16),
+            pltpu.VMEM((X, 224, 640), BF16),
             pltpu.VMEM((Y, 2, X, 128, 256), BF16),
             pltpu.VMEM((Y, 2, X, 128, 256), BF16),
             pltpu.VMEM((Y, X, 128, 256), BF16),
@@ -396,19 +532,45 @@
             pltpu.VMEM((128, 224), F32),
             pltpu.SemaphoreType.DMA((COPIES,)),
             pltpu.SemaphoreType.DMA((COPIES,)),
-            pltpu.SemaphoreType.DMA((4,)),
+            pltpu.SemaphoreType.DMA((7,)),
         ],
         compiler_params=pltpu.CompilerParams(
             collective_id=0, has_side_effects=True, vmem_limit_bytes=52 * 2**20
         ),
-    )(hv, resid, gain, *wgu, *wo, *wd)
-
-
-def spread(piece, x):
-    got = [piece(x)]
+    )(hv, resid, gain, w_gate, w_up, *wgu, w_o, w_down)
+
+
+def cut_kernel(w_gate, w_up, piece1, piece2, piece3, sem):
+    x = lax.axis_index("dp") // Z
+    copies = []
+    for s, piece in enumerate((piece1, piece2, piece3)):
+        start = (9 * lax.rem(x + s + 1, X)) // 2 * 128
+        window = pl.ds(pl.multiple_of(start, 128), 640)
+        for j, w in enumerate((w_gate, w_up)):
+            copies.append(
+                pltpu.make_async_copy(
+                    w.at[:, window], piece.at[:, pl.ds(640 * j, 640)], sem.at[s, j]
+                )
+            )
+    for copy in copies:
+        copy.start()
+    for copy in copies:
+        copy.wait()
+
+
+def spread(w_gate, w_up):
+    hbm = pl.BlockSpec(memory_space=pl.ANY)
+    pieces = pl.pallas_call(
+        cut_kernel,
+        out_shape=[jax.ShapeDtypeStruct((224, 1280), BF16)] * 3,
+        in_specs=[hbm] * 2,
+        out_specs=[hbm] * 3,
+        scratch_shapes=[pltpu.SemaphoreType.DMA((3, 2))],
+    )(w_gate, w_up)
+    got = []
     for s in range(1, X):
         pairs = [(i, (i // Z + s) % X * Z + i % Z) for i in range(X * Z)]
-        got.append(lax.ppermute(piece(lax.rem(x + s, X)), "dp", pairs))
+        got.append(lax.ppermute(pieces[s - 1], "dp", pairs))
     return got
 
 
@@ -430,18 +592,8 @@
     w_up,
     w_down,
 ):
-    x = lax.axis_index("dp") // Z
-
-    def expand_piece(at):
-        gate = lax.dynamic_slice(w_gate, (0, at * 576), (224, 576))
-        up = lax.dynamic_slice(w_up, (0, at * 576), (224, 576))
-        pad = ((0, 0), (0, 64))
-        return jnp.concatenate([jnp.pad(gate, pad), jnp.pad(up, pad)], axis=1)
-
-    wo = spread(lambda at: lax.dynamic_slice(w_o, (at * 512, 0), (512, 224)), x)
-    wgu = spread(expand_piece, x)
-    wd = spread(lambda at: lax.dynamic_slice(w_down, (at * 576, 0), (576, 224)), x)
-    head_values = attend_local(
+    wgu = spread(w_gate, w_up)
+    head_values = attend(
         q_lat,
         q_rope,
         fresh_lat,
@@ -453,7 +605,9 @@
         fresh_len,
         w_uv,
     )
-    return layer(head_values, resid, norm_gain.reshape(1, -1), wgu, wo, wd)
+    return layer(
+        head_values, resid, norm_gain.reshape(1, -1), w_gate, w_up, wgu, w_o.T, w_down.T
+    )
 
 
 def solution(mesh):

time: 249 us -> 202 us (0.81)
  Pallas kernels: 116 us -> 188 us
  matrix products: 44.8 us -> 0 us
  local copies, waits for them, and re-layouts: 41.5 us -> 1.75 us
  other arithmetic: 15.5 us -> 0 us
  waiting for transfers between devices: 17.6 us -> 6.28 us
  starting transfers between devices: 12.7 us -> 5.72 us
    pallas_call x0 -> x2, Pallas kernels: none -> 70.6 us  [the longest x1 53.3 us: spread(): pl.pallas_call(cut_kernel, out_shape=[jax.ShapeDtypeStruct((224, 1280), B...]
    dot_general x6 -> x0, matrix products: 44.8 us -> none  [the longest x1 19.2 us: attend_local(): jnp.einsum('rhl,kl->rhk', queries, keys_lat, preferred_element_type=jnp.f...]
    unnamed x40 -> x7, local copies, waits for them, and re-layouts: 14.2 us -> 1.02 us
    gather x2 -> x0, local copies, waits for them, and re-layouts: 11.8 us -> none  [the longest x1 8.94 us: attend_local(): keys_lat = cache_lat[order].reshape(-1, latent_width)]
    ppermute x9 -> x3, waiting for transfers between devices: 17.6 us -> 6.28 us  [spread(): got.append(lax.ppermute(pieces[s - 1], 'dp', pairs))]
    dynamic_slice x3 -> x0, local copies, waits for them, and re-layouts: 8.89 us -> none  [the longest x1 4.04 us: expand_piece(): up = lax.dynamic_slice(w_up, (0, at * 576), (224, 576))]
    reduce_sum x3 -> x0, other arithmetic: 8.52 us -> none  [the longest x2 8.36 us: attend_local(): denominator = jnp.sum(cache_exp, axis=2) + jnp.sum(fresh_exp, axis=2)]
    ppermute x9 -> x3, starting transfers between devices: 12.7 us -> 5.72 us  [spread(): got.append(lax.ppermute(pieces[s - 1], 'dp', pairs))]
  transfers between devices with their start and end apart: 9 -> 3, of which waited for: 2 -> 1; matrix products, arithmetic and copies ran while one was open for 38% -> 0% of each run, Pallas kernels for 0% -> 9%
where the time goes in v2:
time: 202 us
  Pallas kernels  188 us (93%)
  waiting for transfers between devices  6.28 us (3%)
  starting transfers between devices  5.72 us (3%)
    pallas_call x1, Pallas kernels, layer(): pl.pallas_call(layer_kernel, out_shape=jax.ShapeDtypeStruct((128, 224), B...  117 us
    pallas_call x1, Pallas kernels, spread(): pl.pallas_call(cut_kernel, out_shape=[jax.ShapeDtypeStruct((224, 1280), B...  53.3 us
    pallas_call x1, Pallas kernels, attend(): pl.pallas_call(attend_kernel, out_shape=jax.ShapeDtypeStruct((4, 32, 512)...  17.3 us
    ppermute x3, waiting for transfers between devices, spread(): got.append(lax.ppermute(pieces[s - 1], 'dp', pairs))  6.28 us
    ppermute x3, starting transfers between devices, spread(): got.append(lax.ppermute(pieces[s - 1], 'dp', pairs))  5.72 us
  transfers between devices with their start and end apart: 3, of which 1 were waited for; matrix products, arithmetic and copies ran while one was open for 0% of the time, Pallas kernels for 9%

profile of v2, /device:TPU:1, one launch (start us, length us, event | category | flops | bytes accessed | tf_op | source)
XLA Modules:
  0.0 201.8 jit_solution(14449297852276354494)
XLA Ops:
  0.0 53.3 %shard_map.155 = (bf16[224,1280]{1,0:T(8,128)(2,1)}, bf16[224,1280]{1,0:T(8,128)(2,1)}, bf16[224,1280]{1,0:T(8,128)(2,1)}) custom-call(bf16[224,2304]{1,0:T(8,128)(2,1)} %w_gate.3, bf16[224,2304]{1,0:T(8,128)(2,1)} %w_up.3), custom_call_target="tpu_custom_call" | custom-call | tf_op jit(solution)/shard_map/pallas_call | solution.py:563
  53.3 2.1 %collective-permute-start = (bf16[224,1280]{1,0:T(8,128)(2,1)}, bf16[224,1280]{1,0:T(8,128)(2,1)S(1)}, u32[]{:S(2)}, u32[]{:S(2)}) collective-permute-start(bf16[224,1280]{1,0:T(8,128)(2,1)} %get-tuple-element.8), channel_id=1, source_target_pairs={{0,64},{8,72},{16,80},{24,88},{32,96},{40,104},{48,112},{56,120},{... | collective-permute-start | bytes 1720328 | tf_op jit(solution)/shard_map/ppermute | solution.py:573
  55.4 2.5 %collective-permute-start.1 = (bf16[224,1280]{1,0:T(8,128)(2,1)}, bf16[224,1280]{1,0:T(8,128)(2,1)S(1)}, u32[]{:S(2)}, u32[]{:S(2)}) collective-permute-start(bf16[224,1280]{1,0:T(8,128)(2,1)} %get-tuple-element.9), channel_id=1, source_target_pairs={{0,128},{8,136},{16,144},{24,152},{32,160},{40,168},{48,176},{56,1... | collective-permute-start | bytes 1720328 | tf_op jit(solution)/shard_map/ppermute | solution.py:573
  57.8 0.0 copy-start.1
  57.8 0.0 copy-start.2
  57.8 1.2 collective-permute-start.2
  59.0 17.3 %shard_map.154.hv = bf16[4,32,512]{2,1,0:T(8,128)(2,1)} custom-call(s32[1,2,32]{2,1,0:T(2,128)} %table.1, s32[1,2]{1,0:T(1,128)} %hit.1, s32[1,2]{1,0:T(1,128)} %count.1, bf16[32,8192]{1,0:T(8,128)(2,1)} %q_lat.1, bf16[32,1024]{1,0:T(8,128)(2,1)} %q_rope.1, bf16[32,512]{1,0:T(8,128)(2,1)} %fresh_lat.1, bf16[32,64]{1,0:T(8,128)(2,1)} %fresh_rope.1, ...), custom_call_target="tpu_custom_call" | custom-call | flops 20000000000 | bytes 12582912 | tf_op jit(solution)/shard_map/pallas_call | solution.py:145
  76.3 0.0 copy-done.1
  76.3 0.1 copy.17.resid
  76.4 0.0 copy-done.2
  76.4 0.0 collective-permute-done.wgu1
  76.4 6.3 %collective-permute-done.1.wgu2 = bf16[224,1280]{1,0:T(8,128)(2,1)S(1)} collective-permute-done((bf16[224,1280]{1,0:T(8,128)(2,1)}, bf16[224,1280]{1,0:T(8,128)(2,1)S(1)}, u32[]{:S(2)}, u32[]{:S(2)}) %collective-permute-start.1) | collective-permute-done | bytes 573472 | tf_op jit(solution)/shard_map/ppermute | solution.py:573
  82.7 0.0 collective-permute-done.2.wgu3
  82.7 0.0 copy-start
  82.7 0.9 copy-done
  83.6 117.5 %shard_map.156 = bf16[128,224]{1,0:T(8,128)(2,1)S(1)} custom-call(bf16[4,32,512]{2,1,0:T(8,128)(2,1)S(1)} %copy-done, bf16[128,224]{1,0:T(8,128)(2,1)S(1)} %copy.17.resid, bf16[1,224]{1,0:T(2,128)(2,1)S(1)} %reshape.3.gain, bf16[224,2304]{1,0:T(8,128)(2,1)} %w_gate.3, bf16[224,2304]{1,0:T(8,128)(2,1)} %w_up.3, ...), custom_call_target="tpu_custom_call" | custom-call | tf_op jit(solution)/shard_map/pallas_call | solution.py:511
  201.1 0.7 copy.18
  (1 shorter events, 0.0 us)
Async XLA Ops:
  53.3 23.2 %collective-permute-start = (bf16[224,1280]{1,0:T(8,128)(2,1)}, bf16[224,1280]{1,0:T(8,128)(2,1)S(1)}, u32[]{:S(2)}, u32[]{:S(2)}) collective-permute-start(bf16[224,1280]{1,0:T(8,128)(2,1)} %get-tuple-element.8), channel_id=1, source_target_pairs={{0,64},{8,72},{16,80},{24,88},{32,96},{40,104},{48,112},{56,120},{... | collective-permute-start | bytes 1720328 | tf_op jit(solution)/shard_map/ppermute | solution.py:573
  55.4 27.3 %collective-permute-start.1 = (bf16[224,1280]{1,0:T(8,128)(2,1)}, bf16[224,1280]{1,0:T(8,128)(2,1)S(1)}, u32[]{:S(2)}, u32[]{:S(2)}) collective-permute-start(bf16[224,1280]{1,0:T(8,128)(2,1)} %get-tuple-element.9), channel_id=1, source_target_pairs={{0,128},{8,136},{16,144},{24,152},{32,160},{40,168},{48,176},{56,1... | collective-permute-start | bytes 1720328 | tf_op jit(solution)/shard_map/ppermute | solution.py:573
  57.8 18.5 %copy-start.1 = (bf16[128,224]{0,1:T(8,128)(2,1)S(1)}, bf16[128,224]{0,1:T(8,128)(2,1)}, u32[]{:S(2)}) copy-start(bf16[128,224]{0,1:T(8,128)(2,1)} %param.27) | copy-start | bytes 172036
  57.8 18.6 %copy-start.2 = (bf16[224]{0:T(256)(128)(2,1)S(1)}, bf16[224]{0:T(256)(128)(2,1)}, u32[]{:S(2)}) copy-start(bf16[224]{0:T(256)(128)(2,1)} %param.28) | copy-start | bytes 1348
  57.8 24.9 %collective-permute-start.2 = (bf16[224,1280]{1,0:T(8,128)(2,1)}, bf16[224,1280]{1,0:T(8,128)(2,1)S(1)}, u32[]{:S(2)}, u32[]{:S(2)}) collective-permute-start(bf16[224,1280]{1,0:T(8,128)(2,1)} %get-tuple-element.10), channel_id=1, source_target_pairs={{0,192},{8,200},{16,208},{24,216},{32,224},{40,232},{48,240},{56,2... | collective-permute-start | bytes 1720328 | tf_op jit(solution)/shard_map/ppermute | solution.py:573
  82.7 0.9 copy-start

commit v3 on v2

--- a/solution.py
+++ b/solution.py
@@ -564,7 +564,7 @@
         cut_kernel,
         out_shape=[jax.ShapeDtypeStruct((224, 1280), BF16)] * 3,
         in_specs=[hbm] * 2,
-        out_specs=[hbm] * 3,
+        out_specs=[pl.BlockSpec(memory_space=pltpu.VMEM)] * 3,
         scratch_shapes=[pltpu.SemaphoreType.DMA((3, 2))],
     )(w_gate, w_up)
     got = []

time: 202 us -> 151 us (0.75)
  Pallas kernels: 188 us -> 142 us
  waiting for transfers between devices: 6.28 us -> 1.85 us
    pallas_call x1, Pallas kernels: 53.3 us -> 2.67 us  [spread(): pl.pallas_call(cut_kernel, out_shape=[jax.ShapeDtypeStruct((224, 1280), B...]
    ppermute x3, waiting for transfers between devices: 6.28 us -> 1.85 us  [spread(): got.append(lax.ppermute(pieces[s - 1], 'dp', pairs))]
    pallas_call x1, Pallas kernels: 17.3 us -> 21.7 us  [attend(): pl.pallas_call(attend_kernel, out_shape=jax.ShapeDtypeStruct((4, 32, 512)...]
  transfers between devices with their start and end apart: 3 -> 3, of which waited for: 1 -> 1; matrix products, arithmetic and copies ran while one was open for 0% -> 0% of each run, Pallas kernels for 9% -> 14%
where the time goes in v3:
time: 151 us
  Pallas kernels  142 us (94%)
  starting transfers between devices  5.72 us (4%)
  waiting for transfers between devices  1.85 us (1%)
  local copies, waits for them, and re-layouts  1.75 us (1%)
    pallas_call x1, Pallas kernels, layer(): pl.pallas_call(layer_kernel, out_shape=jax.ShapeDtypeStruct((128, 224), B...  117 us
    pallas_call x1, Pallas kernels, attend(): pl.pallas_call(attend_kernel, out_shape=jax.ShapeDtypeStruct((4, 32, 512)...  21.7 us
    ppermute x3, starting transfers between devices, spread(): got.append(lax.ppermute(pieces[s - 1], 'dp', pairs))  5.72 us
  transfers between devices with their start and end apart: 3, of which 1 were waited for; matrix products, arithmetic and copies ran while one was open for 0% of the time, Pallas kernels for 14%

profile of v3, /device:TPU:1, one launch (start us, length us, event | category | flops | bytes accessed | tf_op | source)
XLA Modules:
  0.0 151.2 jit_solution(7833327433727357068)
XLA Ops:
  0.0 2.7 %shard_map.155 = (bf16[224,1280]{1,0:T(8,128)(2,1)}, bf16[224,1280]{1,0:T(8,128)(2,1)}, bf16[224,1280]{1,0:T(8,128)(2,1)}) custom-call(bf16[224,2304]{1,0:T(8,128)(2,1)} %w_gate.3, bf16[224,2304]{1,0:T(8,128)(2,1)} %w_up.3), custom_call_target="tpu_custom_call" | custom-call | tf_op jit(solution)/shard_map/pallas_call | solution.py:563
  2.7 2.1 %collective-permute-start = (bf16[224,1280]{1,0:T(8,128)(2,1)}, bf16[224,1280]{1,0:T(8,128)(2,1)S(1)}, u32[]{:S(2)}, u32[]{:S(2)}) collective-permute-start(bf16[224,1280]{1,0:T(8,128)(2,1)} %get-tuple-element.8), channel_id=1, source_target_pairs={{0,64},{8,72},{16,80},{24,88},{32,96},{40,104},{48,112},{56,120},{... | collective-permute-start | bytes 1720328 | tf_op jit(solution)/shard_map/ppermute | solution.py:573
  4.8 2.5 %collective-permute-start.1 = (bf16[224,1280]{1,0:T(8,128)(2,1)}, bf16[224,1280]{1,0:T(8,128)(2,1)S(1)}, u32[]{:S(2)}, u32[]{:S(2)}) collective-permute-start(bf16[224,1280]{1,0:T(8,128)(2,1)} %get-tuple-element.9), channel_id=1, source_target_pairs={{0,128},{8,136},{16,144},{24,152},{32,160},{40,168},{48,176},{56,1... | collective-permute-start | bytes 1720328 | tf_op jit(solution)/shard_map/ppermute | solution.py:573
  7.3 0.0 copy-start.1
  7.3 0.0 copy-start.2
  7.3 1.2 collective-permute-start.2
  8.4 21.7 %shard_map.154.hv = bf16[4,32,512]{2,1,0:T(8,128)(2,1)} custom-call(s32[1,2,32]{2,1,0:T(2,128)} %table.1, s32[1,2]{1,0:T(1,128)} %hit.1, s32[1,2]{1,0:T(1,128)} %count.1, bf16[32,8192]{1,0:T(8,128)(2,1)} %q_lat.1, bf16[32,1024]{1,0:T(8,128)(2,1)} %q_rope.1, bf16[32,512]{1,0:T(8,128)(2,1)} %fresh_lat.1, bf16[32,64]{1,0:T(8,128)(2,1)} %fresh_rope.1, ...), custom_call_target="tpu_custom_call" | custom-call | flops 20000000000 | bytes 12582912 | tf_op jit(solution)/shard_map/pallas_call | solution.py:145
  30.1 0.0 copy-done.1
  30.1 0.1 copy.17.resid
  30.2 0.0 copy-done.2
  30.3 0.0 collective-permute-done.wgu1
  30.3 1.8 %collective-permute-done.1.wgu2 = bf16[224,1280]{1,0:T(8,128)(2,1)S(1)} collective-permute-done((bf16[224,1280]{1,0:T(8,128)(2,1)}, bf16[224,1280]{1,0:T(8,128)(2,1)S(1)}, u32[]{:S(2)}, u32[]{:S(2)}) %collective-permute-start.1) | collective-permute-done | bytes 573472 | tf_op jit(solution)/shard_map/ppermute | solution.py:573
  32.1 0.0 collective-permute-done.2.wgu3
  32.1 0.0 copy-start
  32.1 0.9 copy-done
  33.0 117.4 %shard_map.156 = bf16[128,224]{1,0:T(8,128)(2,1)S(1)} custom-call(bf16[4,32,512]{2,1,0:T(8,128)(2,1)S(1)} %copy-done, bf16[128,224]{1,0:T(8,128)(2,1)S(1)} %copy.17.resid, bf16[1,224]{1,0:T(2,128)(2,1)S(1)} %reshape.3.gain, bf16[224,2304]{1,0:T(8,128)(2,1)} %w_gate.3, bf16[224,2304]{1,0:T(8,128)(2,1)} %w_up.3, ...), custom_call_target="tpu_custom_call" | custom-call | tf_op jit(solution)/shard_map/pallas_call | solution.py:511
  150.5 0.7 copy.18
  (1 shorter events, 0.0 us)
Async XLA Ops:
  2.7 27.6 %collective-permute-start = (bf16[224,1280]{1,0:T(8,128)(2,1)}, bf16[224,1280]{1,0:T(8,128)(2,1)S(1)}, u32[]{:S(2)}, u32[]{:S(2)}) collective-permute-start(bf16[224,1280]{1,0:T(8,128)(2,1)} %get-tuple-element.8), channel_id=1, source_target_pairs={{0,64},{8,72},{16,80},{24,88},{32,96},{40,104},{48,112},{56,120},{... | collective-permute-start | bytes 1720328 | tf_op jit(solution)/shard_map/ppermute | solution.py:573
  4.8 27.3 %collective-permute-start.1 = (bf16[224,1280]{1,0:T(8,128)(2,1)}, bf16[224,1280]{1,0:T(8,128)(2,1)S(1)}, u32[]{:S(2)}, u32[]{:S(2)}) collective-permute-start(bf16[224,1280]{1,0:T(8,128)(2,1)} %get-tuple-element.9), channel_id=1, source_target_pairs={{0,128},{8,136},{16,144},{24,152},{32,160},{40,168},{48,176},{56,1... | collective-permute-start | bytes 1720328 | tf_op jit(solution)/shard_map/ppermute | solution.py:573
  7.3 22.9 %copy-start.1 = (bf16[128,224]{0,1:T(8,128)(2,1)S(1)}, bf16[128,224]{0,1:T(8,128)(2,1)}, u32[]{:S(2)}) copy-start(bf16[128,224]{0,1:T(8,128)(2,1)} %param.27) | copy-start | bytes 172036
  7.3 23.0 %copy-start.2 = (bf16[224]{0:T(256)(128)(2,1)S(1)}, bf16[224]{0:T(256)(128)(2,1)}, u32[]{:S(2)}) copy-start(bf16[224]{0:T(256)(128)(2,1)} %param.28) | copy-start | bytes 1348
  7.3 24.9 %collective-permute-start.2 = (bf16[224,1280]{1,0:T(8,128)(2,1)}, bf16[224,1280]{1,0:T(8,128)(2,1)S(1)}, u32[]{:S(2)}, u32[]{:S(2)}) collective-permute-start(bf16[224,1280]{1,0:T(8,128)(2,1)} %get-tuple-element.10), channel_id=1, source_target_pairs={{0,192},{8,200},{16,208},{24,216},{32,224},{40,232},{48,240},{56,2... | collective-permute-start | bytes 1720328 | tf_op jit(solution)/shard_map/ppermute | solution.py:573
  32.1 0.9 copy-start

commit v4 on v3

--- a/solution.py
+++ b/solution.py
@@ -16,7 +16,7 @@
 F32 = jnp.float32
 BF16 = jnp.bfloat16
 CHUNK = 512
-AHEAD = 3
+AHEAD = 4
 LOW = -1e30
 QUERIES = 384
 
@@ -24,7 +24,7 @@
 def attend_kernel(
     table, hit, count, q_lat, q_rope, fresh_lat, fresh_rope, cache_lat, cache_rope, w_uv,
     out,
-    q_all, r_all, shuffle, keys, ropes, peak, mass, acc, w_uv_here, sem, uv_sem,
+    q_all, r_all, shuffle, keys, ropes, peak, mass, acc, w_uv_here, even, odd, sem, uv_sem,
 ):
     pages = CHUNK // 128
     chunks0 = (hit[0, 0] + CHUNK - 1) // CHUNK
@@ -93,37 +93,62 @@
     for j in range(4):
         acc[j] = product[:, 128 * j : 128 * (j + 1)]
 
-    def body(i, _):
-        fetch(i + AHEAD)
+    def ready(i):
+        @pl.when(i < chunks)
+        def _():
+            for j in range(pages):
+                for copy in page_copies(i, j):
+                    copy.wait()
+
+    def window(i):
         r, k = place(i)
         start = pl.multiple_of(r * 128, 128)
-        at = pl.ds(start, QUERIES)
-        for j in range(pages):
-            for copy in page_copies(i, j):
-                copy.wait()
-        block = keys[i]
-        scores = nt(q_all[at, :], block) + jnp.dot(
+        return r, k, start, pl.ds(start, QUERIES)
+
+    def score(i, held):
+        i = jnp.minimum(i, chunks - 1)
+        at = window(i)[3]
+        held[...] = nt(q_all[at, :], keys[i]) + jnp.dot(
             r_all[at, :], ropes[i], preferred_element_type=F32
         )
+
+    def absorb(i, held):
+        own = jnp.minimum(i, chunks - 1)
+        r, k, start, at = window(own)
+        limit = jnp.where(i < chunks, hit[0, r], 0)
         position = k * CHUNK + lax.broadcasted_iota(jnp.int32, (1, CHUNK), 1)
         query = start + lax.broadcasted_iota(jnp.int32, (QUERIES, 1), 0)
         first = r * n0 * 16
         last = jnp.where(r == 0, n0 * 16, 512)
-        column_bias = jnp.where(position < hit[0, r], 0.0, LOW)
+        column_bias = jnp.where(position < limit, 0.0, LOW)
         row_bias = jnp.where((query >= first) & (query < last), 0.0, LOW)
-        scores = scores * scale + column_bias + row_bias
+        scores = held[...] * scale + column_bias + row_bias
         before = peak[at, :]
         top = jnp.maximum(before, jnp.max(scores, axis=1, keepdims=True))
         shrink = jnp.exp2(before - top)
         weight = jnp.exp2(scores - top)
         peak[at, :] = top
         mass[at, :] = mass[at, :] * shrink + jnp.sum(weight, axis=1, keepdims=True)
-        product = jnp.dot(weight.astype(BF16), block, preferred_element_type=F32)
+        product = jnp.dot(weight.astype(BF16), keys[own], preferred_element_type=F32)
         for j in range(4):
             acc[j, at, :] = acc[j, at, :] * shrink + product[:, 128 * j : 128 * (j + 1)]
+
+    ready(0)
+    score(0, even)
+
+    def body(t, _):
+        i = 2 * t
+        fetch(i + AHEAD)
+        fetch(i + 1 + AHEAD)
+        ready(i + 1)
+        ready(i + 2)
+        score(i + 1, odd)
+        absorb(i, even)
+        score(i + 2, even)
+        absorb(i + 1, odd)
         return 0
 
-    lax.fori_loop(0, chunks, body, 0)
+    lax.fori_loop(0, (chunks + 1) // 2, body, 0)
 
     uv_copy.wait()
     inverse = 1.0 / mass[...]
@@ -157,6 +182,8 @@
             pltpu.VMEM((512, 1), F32),
             pltpu.VMEM((4, 512, 128), F32),
             pltpu.VMEM((16, 512, 128), BF16),
+            pltpu.VMEM((QUERIES, CHUNK), F32),
+            pltpu.VMEM((QUERIES, CHUNK), F32),
             pltpu.SemaphoreType.DMA((2, most, CHUNK // 128)),
             pltpu.SemaphoreType.DMA,
         ],
@@ -169,7 +196,7 @@
 
 def layer_kernel(
     hv, resid, gain,
-    w_gate, w_up, wgu1, wgu2, wgu3, w_o, w_down,
+    w_gate, w_up, wgu1, wgu3, w_o, w_down,
     out,
     heads, normed, wgu, wo, wd, part_o, part_d, sib_o, sib_d,
     a1_o, b1_o, ra_o, rb_o, a2_o, b2_o,
@@ -209,10 +236,10 @@
         ),
         pltpu.make_async_copy(w_down.at[:, window(x)], wd.at[0], wsem.at[3]),
     ]
-    for s, block in enumerate((wgu1, wgu2, wgu3)):
+    for i, (s, block) in enumerate(((1, wgu1), (3, wgu3))):
         loads.append(
             pltpu.make_async_copy(
-                block, wgu.at[block_rows(lax.rem(x - s - 1 + X, X)), :], wsem.at[4 + s]
+                block, wgu.at[block_rows(lax.rem(x - s + X, X)), :], wsem.at[4 + i]
             )
         )
     for load in loads:
@@ -319,8 +346,22 @@
         if sub:
             moved[sub].wait_recv()
 
+    unit_moves = []
+    seen = []
+
+    def heads_arrived(zi):
+        seen.append(zi)
+        if len(seen) == 2:
+            there = window(lax.rem(x + 2, X))
+            for j, w in enumerate((w_gate, w_up)):
+                unit_moves.append(
+                    send(
+                        w.at[:, there], wgu.at[block_rows(x), pl.ds(640 * j, 640)], x_of[2]
+                    )
+                )
+
     ring_gather(
-        lambda zi, sub: heads.at[zi, lax.rem(x - sub + X, X)], own_heads, lambda zi: None
+        lambda zi, sub: heads.at[zi, lax.rem(x - sub + X, X)], own_heads, heads_arrived
     )
 
     loads[0].wait()
@@ -388,6 +429,8 @@
 
     for load in loads[1:]:
         load.wait()
+    for copy in unit_moves:
+        copy.wait_recv()
     odd = lax.rem(x, 2)
     edge = pl.multiple_of((1 - odd) * 512, 128)
     lane = lax.broadcasted_iota(jnp.int32, (1, 128), 1)
@@ -511,7 +554,7 @@
     return pl.pallas_call(
         layer_kernel,
         out_shape=jax.ShapeDtypeStruct((128, 224), BF16),
-        in_specs=[vmem] * 3 + [hbm] * 7,
+        in_specs=[vmem] * 3 + [hbm] * 6,
         out_specs=vmem,
         scratch_shapes=[
             pltpu.VMEM((Z, X, 32, 512), BF16),
@@ -532,7 +575,7 @@
             pltpu.VMEM((128, 224), F32),
             pltpu.SemaphoreType.DMA((COPIES,)),
             pltpu.SemaphoreType.DMA((COPIES,)),
-            pltpu.SemaphoreType.DMA((7,)),
+            pltpu.SemaphoreType.DMA((6,)),
         ],
         compiler_params=pltpu.CompilerParams(
             collective_id=0, has_side_effects=True, vmem_limit_bytes=52 * 2**20
@@ -540,16 +583,16 @@
     )(hv, resid, gain, w_gate, w_up, *wgu, w_o, w_down)
 
 
-def cut_kernel(w_gate, w_up, piece1, piece2, piece3, sem):
+def cut_kernel(w_gate, w_up, piece1, piece3, sem):
     x = lax.axis_index("dp") // Z
     copies = []
-    for s, piece in enumerate((piece1, piece2, piece3)):
-        start = (9 * lax.rem(x + s + 1, X)) // 2 * 128
+    for i, (s, piece) in enumerate(((1, piece1), (3, piece3))):
+        start = (9 * lax.rem(x + s, X)) // 2 * 128
         window = pl.ds(pl.multiple_of(start, 128), 640)
         for j, w in enumerate((w_gate, w_up)):
             copies.append(
                 pltpu.make_async_copy(
-                    w.at[:, window], piece.at[:, pl.ds(640 * j, 640)], sem.at[s, j]
+                    w.at[:, window], piece.at[:, pl.ds(640 * j, 640)], sem.at[i, j]
                 )
             )
     for copy in copies:
@@ -562,15 +605,15 @@
     hbm = pl.BlockSpec(memory_space=pl.ANY)
     pieces = pl.pallas_call(
         cut_kernel,
-        out_shape=[jax.ShapeDtypeStruct((224, 1280), BF16)] * 3,
+        out_shape=[jax.ShapeDtypeStruct((224, 1280), BF16)] * 2,
         in_specs=[hbm] * 2,
-        out_specs=[pl.BlockSpec(memory_space=pltpu.VMEM)] * 3,
-        scratch_shapes=[pltpu.SemaphoreType.DMA((3, 2))],
+        out_specs=[pl.BlockSpec(memory_space=pltpu.VMEM)] * 2,
+        scratch_shapes=[pltpu.SemaphoreType.DMA((2, 2))],
     )(w_gate, w_up)
     got = []
-    for s in range(1, X):
+    for s, piece in zip((1, 3), pieces):
         pairs = [(i, (i // Z + s) % X * Z + i % Z) for i in range(X * Z)]
-        got.append(lax.ppermute(pieces[s - 1], "dp", pairs))
+        got.append(lax.ppermute(piece, "dp", pairs))
     return got
 
 

time: 151 us -> 144 us (0.954)
  Pallas kernels: 142 us -> 137 us
  starting transfers between devices: 5.72 us -> 3.5 us
    pallas_call x1, Pallas kernels: 21.7 us -> 9.72 us  [attend(): pl.pallas_call(attend_kernel, out_shape=jax.ShapeDtypeStruct((4, 32, 512)...]
    pallas_call x1, Pallas kernels: 117 us -> 125 us  [layer(): pl.pallas_call(layer_kernel, out_shape=jax.ShapeDtypeStruct((128, 224), B...]
    ppermute x3 -> x2, starting transfers between devices: 5.72 us -> 3.5 us  [spread(): got.append(lax.ppermute(piece, 'dp', pairs))]
  transfers between devices with their start and end apart: 3 -> 2, of which waited for: 1 -> 2; matrix products, arithmetic and copies ran while one was open for 0% -> 0% of each run, Pallas kernels for 14% -> 7%
where the time goes in v4:
time: 144 us
  Pallas kernels  137 us (95%)
  starting transfers between devices  3.5 us (2%)
  waiting for transfers between devices  2.12 us (1%)
  local copies, waits for them, and re-layouts  1.75 us (1%)
    pallas_call x1, Pallas kernels, layer(): pl.pallas_call(layer_kernel, out_shape=jax.ShapeDtypeStruct((128, 224), B...  125 us
    pallas_call x1, Pallas kernels, attend(): pl.pallas_call(attend_kernel, out_shape=jax.ShapeDtypeStruct((4, 32, 512)...  9.72 us
    ppermute x2, starting transfers between devices, spread(): got.append(lax.ppermute(piece, 'dp', pairs))  3.5 us
  transfers between devices with their start and end apart: 2, of which 2 were waited for; matrix products, arithmetic and copies ran while one was open for 0% of the time, Pallas kernels for 7%

profile of v4, /device:TPU:1, one launch (start us, length us, event | category | flops | bytes accessed | tf_op | source)
XLA Modules:
  0.0 144.0 jit_solution(16311563073757059716)
XLA Ops:
  0.0 2.3 %shard_map.155 = (bf16[224,1280]{1,0:T(8,128)(2,1)}, bf16[224,1280]{1,0:T(8,128)(2,1)}) custom-call(bf16[224,2304]{1,0:T(8,128)(2,1)} %w_gate.3, bf16[224,2304]{1,0:T(8,128)(2,1)} %w_up.3), custom_call_target="tpu_custom_call" | custom-call | tf_op jit(solution)/shard_map/pallas_call | solution.py:606
  2.3 2.1 %collective-permute-start = (bf16[224,1280]{1,0:T(8,128)(2,1)}, bf16[224,1280]{1,0:T(8,128)(2,1)S(1)}, u32[]{:S(2)}, u32[]{:S(2)}) collective-permute-start(bf16[224,1280]{1,0:T(8,128)(2,1)} %get-tuple-element.7), channel_id=1, source_target_pairs={{0,64},{8,72},{16,80},{24,88},{32,96},{40,104},{48,112},{56,120},{... | collective-permute-start | bytes 1720328 | tf_op jit(solution)/shard_map/ppermute | solution.py:616
  4.4 0.0 copy-start.1
  4.4 0.0 copy-start.2
  4.4 1.4 collective-permute-start.1
  5.8 9.7 %shard_map.154.hv = bf16[4,32,512]{2,1,0:T(8,128)(2,1)} custom-call(s32[1,2,32]{2,1,0:T(2,128)} %table.1, s32[1,2]{1,0:T(1,128)} %hit.1, s32[1,2]{1,0:T(1,128)} %count.1, bf16[32,8192]{1,0:T(8,128)(2,1)} %q_lat.1, bf16[32,1024]{1,0:T(8,128)(2,1)} %q_rope.1, bf16[32,512]{1,0:T(8,128)(2,1)} %fresh_lat.1, bf16[32,64]{1,0:T(8,128)(2,1)} %fresh_rope.1, ...), custom_call_target="tpu_custom_call" | custom-call | flops 20000000000 | bytes 12582912 | tf_op jit(solution)/shard_map/pallas_call | solution.py:170
  15.5 0.0 copy-done.1
  15.5 0.1 copy.17.resid
  15.6 0.0 copy-done.2
  15.6 0.6 collective-permute-done.wgu1
  16.3 1.5 %collective-permute-done.1.wgu3 = bf16[224,1280]{1,0:T(8,128)(2,1)S(1)} collective-permute-done((bf16[224,1280]{1,0:T(8,128)(2,1)}, bf16[224,1280]{1,0:T(8,128)(2,1)S(1)}, u32[]{:S(2)}, u32[]{:S(2)}) %collective-permute-start.1) | collective-permute-done | bytes 573472 | tf_op jit(solution)/shard_map/ppermute | solution.py:616
  17.8 0.0 copy-start
  17.8 0.9 copy-done
  18.7 124.6 %shard_map.156 = bf16[128,224]{1,0:T(8,128)(2,1)S(1)} custom-call(bf16[4,32,512]{2,1,0:T(8,128)(2,1)S(1)} %copy-done, bf16[128,224]{1,0:T(8,128)(2,1)S(1)} %copy.17.resid, bf16[1,224]{1,0:T(2,128)(2,1)S(1)} %reshape.3.gain, bf16[224,2304]{1,0:T(8,128)(2,1)} %w_gate.3, bf16[224,2304]{1,0:T(8,128)(2,1)} %w_up.3, ...), custom_call_target="tpu_custom_call" | custom-call | tf_op jit(solution)/shard_map/pallas_call | solution.py:554
  143.2 0.7 copy.18
  (1 shorter events, 0.0 us)
Async XLA Ops:
  2.3 14.0 %collective-permute-start = (bf16[224,1280]{1,0:T(8,128)(2,1)}, bf16[224,1280]{1,0:T(8,128)(2,1)S(1)}, u32[]{:S(2)}, u32[]{:S(2)}) collective-permute-start(bf16[224,1280]{1,0:T(8,128)(2,1)} %get-tuple-element.7), channel_id=1, source_target_pairs={{0,64},{8,72},{16,80},{24,88},{32,96},{40,104},{48,112},{56,120},{... | collective-permute-start | bytes 1720328 | tf_op jit(solution)/shard_map/ppermute | solution.py:616
  4.4 11.1 %copy-start.1 = (bf16[128,224]{0,1:T(8,128)(2,1)S(1)}, bf16[128,224]{0,1:T(8,128)(2,1)}, u32[]{:S(2)}) copy-start(bf16[128,224]{0,1:T(8,128)(2,1)} %param.27) | copy-start | bytes 172036
  4.4 11.2 %copy-start.2 = (bf16[224]{0:T(256)(128)(2,1)S(1)}, bf16[224]{0:T(256)(128)(2,1)}, u32[]{:S(2)}) copy-start(bf16[224]{0:T(256)(128)(2,1)} %param.28) | copy-start | bytes 1348
  4.4 13.4 %collective-permute-start.1 = (bf16[224,1280]{1,0:T(8,128)(2,1)}, bf16[224,1280]{1,0:T(8,128)(2,1)S(1)}, u32[]{:S(2)}, u32[]{:S(2)}) collective-permute-start(bf16[224,1280]{1,0:T(8,128)(2,1)} %get-tuple-element.8), channel_id=1, source_target_pairs={{0,192},{8,200},{16,208},{24,216},{32,224},{40,232},{48,240},{56,2... | collective-permute-start | bytes 1720328 | tf_op jit(solution)/shard_map/ppermute | solution.py:616
  17.8 0.9 copy-start

commit v5 on v4

--- a/solution.py
+++ b/solution.py
@@ -287,48 +287,86 @@
             got["r" if sub < 2 else "l", 3, sub].wait_recv()
         arrived(lax.rem(z + 4, Z))
 
-    def reduce_scatter(part, sib, a1, b1, ra, rb, a2, b2):
-        swaps = []
-        for k in (1, 2, 3, 0):
+    def nt(a, b):
+        return lax.dot_general(a, b, (((1,), (1,)), ((), ())), preferred_element_type=F32)
+
+    def scatter(part, a1, b1, ra, rb, a2, b2, in_turn):
+        stage_a = []
+        base = len(sent)
+
+        def to_row(k, yk):
+            return pltpu.make_async_remote_copy(
+                src_ref=part.at[yk, c, :, pl.ds(64, 64), :],
+                dst_ref=b1.at[k - 1],
+                send_sem=ssem.at[base + k - 1],
+                recv_sem=rsem.at[base + k - 1],
+                device_id=(dp, yk * 2 + c),
+                device_id_type=MESH,
+            )
+
+        stage_b = [to_row(k, lax.rem(y + k, Y)) for k in (1, 2, 3)]
+        sent.extend(stage_b)
+
+        def first(yk):
+            k = lax.rem(yk - y + Y, Y)
+
+            @pl.when(k != 0)
+            def _():
+                to_row(k, yk).start()
+
+            for j in (1, 2, 3):
+                stage_a.append(
+                    send(
+                        part.at[yk, c, lax.rem(x + j, X), pl.ds(0, 64), :],
+                        a1.at[j - 1, yk],
+                        x_of[j],
+                    )
+                )
+
+        def second_a(k):
             yk = lax.rem(y + k, Y)
-            swaps.append((k, yk, send(part.at[yk, 1 - c], sib.at[k], sibling)))
-        stage_b, stage_a = [], []
-        for k, yk, copy in swaps:
-            copy.wait_recv()
-            part[yk, c] = part[yk, c] + sib[k]
-            if k:
-                stage_b.append(send(part.at[yk, c, :, pl.ds(64, 64), :], b1.at[k - 1], y_of[k]))
-        for k in (1, 2, 3):
-            xk = lax.rem(x + k, X)
-            stage_a.append(send(part.at[:, c, xk, pl.ds(0, 64), :], a1.at[k - 1], x_of[k]))
-        for copy in stage_b:
-            copy.wait_recv()
-        total = part[y, c, :, 64:128, :].astype(F32)
-        for k in range(3):
-            total = total + b1[k].astype(F32)
-        rb[...] = total.astype(BF16)
-        last_b = [
-            send(rb.at[lax.rem(x + k, X)], b2.at[k - 1], x_of[k]) for k in (1, 2, 3)
-        ]
-        for copy in stage_a:
-            copy.wait_recv()
-        total = part[:, c, x, 0:64, :].astype(F32)
-        for k in range(3):
-            total = total + a1[k].astype(F32)
-        ra[...] = total.astype(BF16)
-        last_a = [
-            send(ra.at[lax.rem(y + k, Y)], a2.at[k - 1], y_of[k]) for k in (1, 2, 3)
-        ]
-        for copy in last_a + last_b:
-            copy.wait_recv()
-        half_a = ra[y].astype(F32)
-        half_b = rb[x].astype(F32)
-        for k in range(3):
-            half_a = half_a + a2[k].astype(F32)
-            half_b = half_b + b2[k].astype(F32)
-        return half_a[:, :224], half_b[:, :224]
-
-    heads[z, x] = hv[x]
+            total = part[yk, c, x, 0:64, :].astype(F32)
+            for j in (1, 2, 3):
+                if in_turn:
+                    stage_a[3 * ((k - 1) % Y) + j - 1].wait_recv()
+                total = total + a1[j - 1, yk].astype(F32)
+            if k == 0:
+                return total
+            ra[k] = total.astype(BF16)
+            return send(ra.at[k], a2.at[k - 1], y_of[k])
+
+        def second_b(j):
+            xj = lax.rem(x + j, X)
+            total = part[y, c, xj, 64:128, :].astype(F32)
+            for k in range(3):
+                total = total + b1[k, xj].astype(F32)
+            if j == 0:
+                return total
+            rb[j] = total.astype(BF16)
+            return send(rb.at[j], b2.at[j - 1], x_of[j])
+
+        def finish():
+            if not in_turn:
+                for copy in stage_a:
+                    copy.wait_recv()
+            last_a = [second_a(k) for k in (1, 2, 3)]
+            for copy in stage_b:
+                copy.wait_recv()
+            last_b = [second_b(j) for j in (1, 2, 3)]
+            half_b = second_b(0)
+            half_a = second_a(0)
+            for k in range(3):
+                last_a[k].wait_recv()
+                half_a = half_a + a2[k].astype(F32)
+            for k in range(3):
+                last_b[k].wait_recv()
+                half_b = half_b + b2[k].astype(F32)
+            return half_a[:, :224], half_b[:, :224]
+
+        return first, finish
+
+    own_heads_copy = pltpu.make_async_copy(hv.at[x], heads.at[z, x], wsem.at[6])
+    own_heads_copy.start()
     moved = [None] + [
         send(hv.at[lax.rem(x + k, X)], heads.at[z, x], x_of[k]) for k in (1, 2, 3)
     ]
@@ -345,6 +383,8 @@
     def own_heads(sub):
         if sub:
             moved[sub].wait_recv()
+        else:
+            own_heads_copy.wait()
 
     unit_moves = []
     seen = []
@@ -368,19 +408,20 @@
     for copy in wo_moves:
         copy.wait_recv()
 
-    def nt(a, b):
-        return lax.dot_general(a, b, (((1,), (1,)), ((), ())), preferred_element_type=F32)
-
-    def project(j, _):
-        rows = heads[:, j].reshape(Z * 32, 512)
+    swaps = []
+    for k in (1, 2, 3, 0):
+        yk = lax.rem(y + k, Y)
+        rows = heads[:, yk].reshape(Z * 32, 512)
         for s in range(X):
             product = nt(rows, wo[s]).astype(BF16)
-            part_o[j, :, lax.rem(x - s + X, X), :, 0:224] = product.reshape(2, 128, 224)
-        return 0
-
-    lax.fori_loop(0, Y, project, 0)
-
-    halves = reduce_scatter(part_o, sib_o, a1_o, b1_o, ra_o, rb_o, a2_o, b2_o)
+            part_o[yk, :, lax.rem(x - s + X, X), :, 0:224] = product.reshape(2, 128, 224)
+        swaps.append((k, yk, send(part_o.at[yk, 1 - c], sib_o.at[k], sibling)))
+    first, finish = scatter(part_o, a1_o, b1_o, ra_o, rb_o, a2_o, b2_o, True)
+    for k, yk, copy in swaps:
+        copy.wait_recv()
+        part_o[yk, c] = part_o[yk, c] + sib_o[k]
+        first(yk)
+    halves = finish()
 
     width = pl.ds(pl.multiple_of(x * 256, 256), 256)
     for h, attended in enumerate(halves):
@@ -526,10 +567,45 @@
 
     for copy in wd_moves:
         copy.wait_recv()
-    ring_gather(lambda zi, sub: hidden.at[zi, sub_rows(sub)], own_hidden, contract)
-    contract(z)
-
-    halves = reduce_scatter(part_d, sib_d, a1_d, b1_d, ra_d, rb_d, a2_d, b2_d)
+    first, finish = scatter(part_d, a1_d, b1_d, ra_d, rb_d, a2_d, b2_d, False)
+
+    def in_order(parity):
+        odd_hops = lax.rem(z + 1 + parity, 2) == 0
+        steps = ((1, 0), (Z - 1, 2), (3, Z - 2), (Z - 3, 4))
+        return [lax.rem(z + jnp.where(odd_hops, a, b), Z) // 2 for a, b in steps]
+
+    to_sibling, from_sibling = in_order(1 - c), in_order(c)
+    swaps = []
+    met = []
+
+    def swap(slot):
+        swaps.append(send(part_d.at[to_sibling[slot], 1 - c], sib_d.at[slot], sibling))
+
+    def add_swapped(slot):
+        swaps[slot].wait_recv()
+        at = from_sibling[slot]
+        part_d[at, c] = part_d[at, c] + sib_d[slot]
+        first(at)
+
+    def hidden_arrived(zi):
+        if not met:
+            contract(z)
+        contract(zi)
+        met.append(zi)
+        if len(met) == 4:
+            swap(0)
+            swap(1)
+        elif len(met) == 6:
+            swap(2)
+            add_swapped(0)
+            add_swapped(1)
+        elif len(met) == 7:
+            swap(3)
+            add_swapped(2)
+
+    ring_gather(lambda zi, sub: hidden.at[zi, sub_rows(sub)], own_hidden, hidden_arrived)
+    add_swapped(3)
+    halves = finish()
     for h, mlp in enumerate(halves):
         at = pl.ds(64 * h, 64)
         out[at, :] = (stream[at, :] + mlp).astype(BF16)
@@ -537,7 +613,7 @@
         copy.wait_send()
 
 
-COPIES = 176
+COPIES = 200
 
 
 def layer(hv, resid, gain, w_gate, w_up, wgu, w_o, w_down):
@@ -554,7 +630,7 @@
     return pl.pallas_call(
         layer_kernel,
         out_shape=jax.ShapeDtypeStruct((128, 224), BF16),
-        in_specs=[vmem] * 3 + [hbm] * 6,
+        in_specs=[hbm] + [vmem] * 2 + [hbm] * 6,
         out_specs=vmem,
         scratch_shapes=[
             pltpu.VMEM((Z, X, 32, 512), BF16),
@@ -575,7 +651,7 @@
             pltpu.VMEM((128, 224), F32),
             pltpu.SemaphoreType.DMA((COPIES,)),
             pltpu.SemaphoreType.DMA((COPIES,)),
-            pltpu.SemaphoreType.DMA((6,)),
+            pltpu.SemaphoreType.DMA((7,)),
         ],
         compiler_params=pltpu.CompilerParams(
             collective_id=0, has_side_effects=True, vmem_limit_bytes=52 * 2**20

time: 144 us -> 139 us (0.965); the launches traced: 144 us -> 137 us
  Pallas kernels: 137 us -> 131 us
  waiting for transfers between devices: 2.12 us -> 0.01 us
    pallas_call x1, Pallas kernels: 125 us -> 114 us  [layer(): pl.pallas_call(layer_kernel, out_shape=jax.ShapeDtypeStruct((128, 224), B...]
    pallas_call x1, Pallas kernels: 9.72 us -> 15.4 us  [attend(): pl.pallas_call(attend_kernel, out_shape=jax.ShapeDtypeStruct((4, 32, 512)...]
    ppermute x2, waiting for transfers between devices: 2.12 us -> 0.01 us  [spread(): got.append(lax.ppermute(piece, 'dp', pairs))]
  transfers between devices with their start and end apart: 2 -> 2, of which waited for: 2 -> 0; matrix products, arithmetic and copies ran while one was open for 0% -> 0% of each run, Pallas kernels for 7% -> 11%
where the time goes in v5:
time: 139 us; the launch traced here: 137 us
  Pallas kernels  131 us (94%)
  starting transfers between devices  3.5 us (3%)
  local copies, waits for them, and re-layouts  1.74 us (1%)
    pallas_call x1, Pallas kernels, layer(): pl.pallas_call(layer_kernel, out_shape=jax.ShapeDtypeStruct((128, 224), B...  114 us
    pallas_call x1, Pallas kernels, attend(): pl.pallas_call(attend_kernel, out_shape=jax.ShapeDtypeStruct((4, 32, 512)...  15.4 us
    ppermute x2, starting transfers between devices, spread(): got.append(lax.ppermute(piece, 'dp', pairs))  3.5 us
  transfers between devices with their start and end apart: 2, of which 0 were waited for; matrix products, arithmetic and copies ran while one was open for 0% of the time, Pallas kernels for 11%

profile of v5, /device:TPU:1, one launch (start us, length us, event | category | flops | bytes accessed | tf_op | source)
XLA Modules:
  0.0 136.7 jit_solution(16059402065528577008)
XLA Ops:
  0.0 2.3 %shard_map.155 = (bf16[224,1280]{1,0:T(8,128)(2,1)}, bf16[224,1280]{1,0:T(8,128)(2,1)}) custom-call(bf16[224,2304]{1,0:T(8,128)(2,1)} %w_gate.3, bf16[224,2304]{1,0:T(8,128)(2,1)} %w_up.3), custom_call_target="tpu_custom_call" | custom-call | tf_op jit(solution)/shard_map/pallas_call | solution.py:682
  2.3 2.1 %collective-permute-start = (bf16[224,1280]{1,0:T(8,128)(2,1)}, bf16[224,1280]{1,0:T(8,128)(2,1)S(1)}, u32[]{:S(2)}, u32[]{:S(2)}) collective-permute-start(bf16[224,1280]{1,0:T(8,128)(2,1)} %get-tuple-element.7), channel_id=1, source_target_pairs={{0,64},{8,72},{16,80},{24,88},{32,96},{40,104},{48,112},{56,120},{... | collective-permute-start | bytes 1720328 | tf_op jit(solution)/shard_map/ppermute | solution.py:692
  4.4 0.0 copy-start.1
  4.4 0.0 copy-start.2
  4.4 1.4 %collective-permute-start.1 = (bf16[224,1280]{1,0:T(8,128)(2,1)}, bf16[224,1280]{1,0:T(8,128)(2,1)S(1)}, u32[]{:S(2)}, u32[]{:S(2)}) collective-permute-start(bf16[224,1280]{1,0:T(8,128)(2,1)} %get-tuple-element.8), channel_id=1, source_target_pairs={{0,192},{8,200},{16,208},{24,216},{32,224},{40,232},{48,240},{56,2... | collective-permute-start | bytes 1720328 | tf_op jit(solution)/shard_map/ppermute | solution.py:692
  5.8 15.4 %shard_map.154.hv = bf16[4,32,512]{2,1,0:T(8,128)(2,1)} custom-call(s32[1,2,32]{2,1,0:T(2,128)} %table.1, s32[1,2]{1,0:T(1,128)} %hit.1, s32[1,2]{1,0:T(1,128)} %count.1, bf16[32,8192]{1,0:T(8,128)(2,1)} %q_lat.1, bf16[32,1024]{1,0:T(8,128)(2,1)} %q_rope.1, bf16[32,512]{1,0:T(8,128)(2,1)} %fresh_lat.1, bf16[32,64]{1,0:T(8,128)(2,1)} %fresh_rope.1, ...), custom_call_target="tpu_custom_call" | custom-call | flops 20000000000 | bytes 12582912 | tf_op jit(solution)/shard_map/pallas_call | solution.py:170
  21.2 0.0 copy-done.1
  21.2 0.1 copy.17.resid
  21.3 0.0 copy-done.2
  21.3 0.0 collective-permute-done.wgu1
  21.4 0.0 collective-permute-done.1.wgu3
  21.4 0.0 copy-start
  21.4 0.9 copy-done
  22.3 113.7 %shard_map.156 = bf16[128,224]{1,0:T(8,128)(2,1)S(1)} custom-call(bf16[4,32,512]{2,1,0:T(8,128)(2,1)S(1)} %copy-done, bf16[128,224]{1,0:T(8,128)(2,1)S(1)} %copy.17.resid, bf16[1,224]{1,0:T(2,128)(2,1)S(1)} %reshape.3.gain, bf16[224,2304]{1,0:T(8,128)(2,1)} %w_gate.3, bf16[224,2304]{1,0:T(8,128)(2,1)} %w_up.3, ...), custom_call_target="tpu_custom_call" | custom-call | tf_op jit(solution)/shard_map/pallas_call | solution.py:630
  136.0 0.7 copy.18
  (1 shorter events, 0.0 us)
Async XLA Ops:
  2.3 19.1 %collective-permute-start = (bf16[224,1280]{1,0:T(8,128)(2,1)}, bf16[224,1280]{1,0:T(8,128)(2,1)S(1)}, u32[]{:S(2)}, u32[]{:S(2)}) collective-permute-start(bf16[224,1280]{1,0:T(8,128)(2,1)} %get-tuple-element.7), channel_id=1, source_target_pairs={{0,64},{8,72},{16,80},{24,88},{32,96},{40,104},{48,112},{56,120},{... | collective-permute-start | bytes 1720328 | tf_op jit(solution)/shard_map/ppermute | solution.py:692
  4.4 16.8 %copy-start.1 = (bf16[128,224]{0,1:T(8,128)(2,1)S(1)}, bf16[128,224]{0,1:T(8,128)(2,1)}, u32[]{:S(2)}) copy-start(bf16[128,224]{0,1:T(8,128)(2,1)} %param.27) | copy-start | bytes 172036
  4.4 16.9 %copy-start.2 = (bf16[224]{0:T(256)(128)(2,1)S(1)}, bf16[224]{0:T(256)(128)(2,1)}, u32[]{:S(2)}) copy-start(bf16[224]{0:T(256)(128)(2,1)} %param.28) | copy-start | bytes 1348
  4.4 17.0 %collective-permute-start.1 = (bf16[224,1280]{1,0:T(8,128)(2,1)}, bf16[224,1280]{1,0:T(8,128)(2,1)S(1)}, u32[]{:S(2)}, u32[]{:S(2)}) collective-permute-start(bf16[224,1280]{1,0:T(8,128)(2,1)} %get-tuple-element.8), channel_id=1, source_target_pairs={{0,192},{8,200},{16,208},{24,216},{32,224},{40,232},{48,240},{56,2... | collective-permute-start | bytes 1720328 | tf_op jit(solution)/shard_map/ppermute | solution.py:692
  21.4 0.9 copy-start

commit v6 on v5

--- a/solution.py
+++ b/solution.py
@@ -201,7 +201,7 @@
     heads, normed, wgu, wo, wd, part_o, part_d, sib_o, sib_d,
     a1_o, b1_o, ra_o, rb_o, a2_o, b2_o,
     a1_d, b1_d, ra_d, rb_d, a2_d, b2_d,
-    terms, from_left, from_right, hidden, stream,
+    terms, from_left, from_right, hidden, stream, squares_out, squares_in, scale,
     ssem, rsem, wsem,
 ):
     dp, tensor = lax.axis_index("dp"), lax.axis_index("tensor")
@@ -218,35 +218,39 @@
     y_of = [near(dy=k) for k in range(Y)]
     right, left, sibling = near(dz=1), near(dz=Z - 1), near(dc=1)
 
-    def window(xk):
-        return pl.ds(pl.multiple_of((9 * xk) // 2 * 128, 128), 640)
+    def whole_tiles(xk):
+        start = ((9 * xk) // 2 + lax.rem(xk, 2)) * 128
+        return pl.ds(pl.multiple_of(start, 128), 512)
+
+    def half_tile(xk):
+        start = ((9 * xk) // 2 + 4 * (1 - lax.rem(xk, 2))) * 128
+        return pl.ds(pl.multiple_of(start, 128), 128)
 
     def block_rows(xk):
         return pl.ds(pl.multiple_of(xk * 256, 256), 224)
 
+    def unit_blocks(xk):
+        for j, w in enumerate((w_gate, w_up)):
+            yield w.at[:, whole_tiles(xk)], wgu.at[block_rows(x), pl.ds(512 * j, 512)]
+            yield w.at[:, half_tile(xk)], wgu.at[block_rows(x), pl.ds(1024 + 128 * j, 128)]
+
+    def down_blocks(xk, at):
+        yield w_down.at[:, whole_tiles(xk)], wd.at[at, :, pl.ds(0, 512)]
+        yield w_down.at[:, half_tile(xk)], wd.at[at, :, pl.ds(512, 128)]
+
+    pairs = [(w_o.at[:, pl.ds(pl.multiple_of(x * 512, 512), 512)], wo.at[0])]
+    pairs += [*unit_blocks(x), *down_blocks(x, 0)]
+    for s, block in ((1, wgu1), (3, wgu3)):
+        pairs.append((block, wgu.at[block_rows(lax.rem(x - s + X, X)), :]))
     loads = [
-        pltpu.make_async_copy(
-            w_o.at[:, pl.ds(pl.multiple_of(x * 512, 512), 512)], wo.at[0], wsem.at[0]
-        ),
-        pltpu.make_async_copy(
-            w_gate.at[:, window(x)], wgu.at[block_rows(x), pl.ds(0, 640)], wsem.at[1]
-        ),
-        pltpu.make_async_copy(
-            w_up.at[:, window(x)], wgu.at[block_rows(x), pl.ds(640, 640)], wsem.at[2]
-        ),
-        pltpu.make_async_copy(w_down.at[:, window(x)], wd.at[0], wsem.at[3]),
+        pltpu.make_async_copy(src, dst, wsem.at[i]) for i, (src, dst) in enumerate(pairs)
     ]
-    for i, (s, block) in enumerate(((1, wgu1), (3, wgu3))):
-        loads.append(
-            pltpu.make_async_copy(
-                block, wgu.at[block_rows(lax.rem(x - s + X, X)), :], wsem.at[4 + i]
-            )
-        )
     for load in loads:
         load.start()
 
     barrier = pltpu.get_barrier_semaphore()
-    partners = x_of[1:] + y_of[1:] + [right, left, sibling]
+    z_of = [near(dz=k) for k in range(Z)]
+    partners = x_of[1:] + y_of[1:] + z_of[1:] + [sibling]
     for device in partners:
         pl.semaphore_signal(barrier, inc=1, device_id=device, device_id_type=MESH)
     pl.semaphore_wait(barrier, len(partners))
@@ -365,7 +369,7 @@
 
         return first, finish
 
-    own_heads_copy = pltpu.make_async_copy(hv.at[x], heads.at[z, x], wsem.at[6])
+    own_heads_copy = pltpu.make_async_copy(hv.at[x], heads.at[z, x], wsem.at[9])
     own_heads_copy.start()
     moved = [None] + [
         send(hv.at[lax.rem(x + k, X)], heads.at[z, x], x_of[k]) for k in (1, 2, 3)
@@ -392,13 +396,8 @@
     def heads_arrived(zi):
         seen.append(zi)
         if len(seen) == 2:
-            there = window(lax.rem(x + 2, X))
-            for j, w in enumerate((w_gate, w_up)):
-                unit_moves.append(
-                    send(
-                        w.at[:, there], wgu.at[block_rows(x), pl.ds(640 * j, 640)], x_of[2]
-                    )
-                )
+            for src, dst in unit_blocks(lax.rem(x + 2, X)):
+                unit_moves.append(send(src, dst, x_of[2]))
 
     ring_gather(
         lambda zi, sub: heads.at[zi, lax.rem(x - sub + X, X)], own_heads, heads_arrived
@@ -473,23 +472,29 @@
     for copy in unit_moves:
         copy.wait_recv()
     odd = lax.rem(x, 2)
-    edge = pl.multiple_of((1 - odd) * 512, 128)
-    lane = lax.broadcasted_iota(jnp.int32, (1, 128), 1)
-    mine = (lane >= 64 * odd) & (lane < 64 + 64 * odd)
-    for start in (edge, 640 + edge):
-        tile = pl.ds(pl.multiple_of(start, 128), 128)
-        wgu[:, tile] = jnp.where(mine, wgu[:, tile].astype(F32), 0.0).astype(BF16)
-    row = lax.broadcasted_iota(jnp.int32, (32, 1280), 0)
-    lane = lax.broadcasted_iota(jnp.int32, (32, 1280), 1)
-    tail = jnp.where((row < 2) & (lane == 576 * (1 - odd)), 1.0, 0.0).astype(BF16)
+    low = lax.broadcasted_iota(jnp.int32, (1, 128), 1) < 64
     for q in range(X):
-        wgu[256 * q + 224 : 256 * q + 256, :] = tail
+        at = pl.ds(256 * q, 256)
+        gate_half = wgu[at, 1024:1152].astype(F32)
+        up_half = wgu[at, 1152:1280].astype(F32)
+        even_mix = jnp.where(low, gate_half, pltpu.roll(up_half, 64, 1))
+        odd_mix = jnp.where(low, pltpu.roll(gate_half, 64, 1), up_half)
+        wgu[at, 1024:1152] = jnp.where(odd == 1, odd_mix, even_mix).astype(BF16)
+        wgu[256 * q + 224 : 256 * q + 256, :] = jnp.zeros((32, 1280), BF16)
     for copy in over:
         copy.wait_recv()
 
+    lane = lax.broadcasted_iota(jnp.int32, (8, X * 256), 1)
+    pick = jnp.where(lax.rem(lane, 256) // 2 == 112, 1.0, 0.0).astype(BF16)
+    for b in range(Z):
+        squares_out[b] = nt(pick, normed[b // 2, b % 2])
+    square_moves = [
+        send(squares_out.at[lax.rem(z + k, Z)], squares_in.at[k], z_of[k]) for k in range(1, Z)
+    ]
+
     def expand(b):
         rows = normed[b // 2, lax.rem(b, 2)]
-        terms[b] = jnp.dot(rows, wgu[...], preferred_element_type=F32).astype(BF16)
+        terms[b] = jnp.dot(rows, wgu[:, 0:1152], preferred_element_type=F32).astype(BF16)
 
     def block_at(j):
         far = 4 - (j + 1) // 2
@@ -526,9 +531,10 @@
         got["l", 1, i] = send(
             terms.at[lax.rem(z + 5, Z), sub_rows(i)], from_right.at[1, sub_rows(i)], left
         )
-    wd_moves = [
-        send(w_down.at[:, window(lax.rem(x + k, X))], wd.at[k], x_of[k]) for k in (1, 2, 3)
-    ]
+    wd_moves = []
+    for k in (1, 2, 3):
+        for src, dst in down_blocks(lax.rem(x + k, X), k):
+            wd_moves.append(send(src, dst, x_of[k]))
     expand_range(3, 8)
 
     def pass_on(step, sub, way):
@@ -547,6 +553,15 @@
             pass_on(step, (i + 2) % 4, "r")
             pass_on(step, i, "l")
 
+    squares = squares_out[z]
+    for k, copy in enumerate(square_moves):
+        copy.wait_recv()
+        squares = squares + squares_in[k + 1]
+    row = lax.broadcasted_iota(jnp.int32, (128, 128), 0)
+    lane = lax.broadcasted_iota(jnp.int32, (128, 128), 1)
+    diagonal = jnp.where(row == lane, jnp.broadcast_to(squares[0:1, :], (128, 128)), 0.0)
+    scale[...] = lax.rsqrt(jnp.sum(diagonal, axis=1, keepdims=True) * (1.0 / D) + EPS)
+
     def own_hidden(sub):
         at = sub_rows(sub)
         got["r", 3, sub].wait_recv()
@@ -554,10 +569,14 @@
         total = (
             terms[z, at].astype(F32) + from_left[3, at].astype(F32) + from_right[3, at].astype(F32)
         )
-        squares = jnp.where(odd == 1, total[:, 0:1], total[:, 576:577])
-        scale = lax.rsqrt(squares * (1.0 / D) + EPS)
-        gate, up = total[:, :640] * scale, total[:, 640:] * scale
-        hidden[z, at] = (gate / (1.0 + jnp.exp(-gate)) * up).astype(BF16)
+        factor = scale[at, :]
+        gate, up = total[:, :512] * factor, total[:, 512:1024] * factor
+        mixed = total[:, 1024:] * factor
+        half = mixed / (1.0 + jnp.exp(-mixed)) * pltpu.roll(mixed, 64, 1)
+        half = jnp.where(low, half, 0.0)
+        half = jnp.where(odd == 1, pltpu.roll(half, 64, 1), half)
+        hidden[z, at, 0:512] = (gate / (1.0 + jnp.exp(-gate)) * up).astype(BF16)
+        hidden[z, at, 512:640] = half.astype(BF16)
 
     def contract(b):
         rows = hidden[b]
@@ -613,7 +632,7 @@
         copy.wait_send()
 
 
-COPIES = 200
+COPIES = 240
 
 
 def layer(hv, resid, gain, w_gate, w_up, wgu, w_o, w_down):
@@ -630,7 +649,7 @@
     return pl.pallas_call(
         layer_kernel,
         out_shape=jax.ShapeDtypeStruct((128, 224), BF16),
-        in_specs=[hbm] + [vmem] * 2 + [hbm] * 6,
+        in_specs=[pl.BlockSpec(memory_space=pltpu.HBM)] + [vmem] * 2 + [hbm] * 6,
         out_specs=vmem,
         scratch_shapes=[
             pltpu.VMEM((Z, X, 32, 512), BF16),
@@ -644,14 +663,17 @@
             pltpu.VMEM((Y, X, 128, 256), BF16),
             *halves,
             *halves,
-            pltpu.VMEM((Z, 128, 1280), BF16),
-            pltpu.VMEM((4, 128, 1280), BF16),
-            pltpu.VMEM((4, 128, 1280), BF16),
+            pltpu.VMEM((Z, 128, 1152), BF16),
+            pltpu.VMEM((4, 128, 1152), BF16),
+            pltpu.VMEM((4, 128, 1152), BF16),
             pltpu.VMEM((Z, 128, 640), BF16),
             pltpu.VMEM((128, 224), F32),
+            pltpu.VMEM((Z, 8, 128), F32),
+            pltpu.VMEM((Z, 8, 128), F32),
+            pltpu.VMEM((128, 1), F32),
             pltpu.SemaphoreType.DMA((COPIES,)),
             pltpu.SemaphoreType.DMA((COPIES,)),
-            pltpu.SemaphoreType.DMA((7,)),
+            pltpu.SemaphoreType.DMA((11,)),
         ],
         compiler_params=pltpu.CompilerParams(
             collective_id=0, has_side_effects=True, vmem_limit_bytes=52 * 2**20
@@ -663,12 +685,19 @@
     x = lax.axis_index("dp") // Z
     copies = []
     for i, (s, piece) in enumerate(((1, piece1), (3, piece3))):
-        start = (9 * lax.rem(x + s, X)) // 2 * 128
-        window = pl.ds(pl.multiple_of(start, 128), 640)
+        there = lax.rem(x + s, X)
+        first, odd = (9 * there) // 2, lax.rem(there, 2)
+        whole = pl.ds(pl.multiple_of((first + odd) * 128, 128), 512)
+        half = pl.ds(pl.multiple_of((first + 4 * (1 - odd)) * 128, 128), 128)
         for j, w in enumerate((w_gate, w_up)):
             copies.append(
                 pltpu.make_async_copy(
-                    w.at[:, window], piece.at[:, pl.ds(640 * j, 640)], sem.at[i, j]
+                    w.at[:, whole], piece.at[:, pl.ds(512 * j, 512)], sem.at[i, 2 * j]
+                )
+            )
+            copies.append(
+                pltpu.make_async_copy(
+                    w.at[:, half], piece.at[:, pl.ds(1024 + 128 * j, 128)], sem.at[i, 2 * j + 1]
                 )
             )
     for copy in copies:
@@ -684,7 +713,7 @@
         out_shape=[jax.ShapeDtypeStruct((224, 1280), BF16)] * 2,
         in_specs=[hbm] * 2,
         out_specs=[pl.BlockSpec(memory_space=pltpu.VMEM)] * 2,
-        scratch_shapes=[pltpu.SemaphoreType.DMA((2, 2))],
+        scratch_shapes=[pltpu.SemaphoreType.DMA((2, 4))],
     )(w_gate, w_up)
     got = []
     for s, piece in zip((1, 3), pieces):

time: 139 us -> 145 us (1.043)
  Pallas kernels: 131 us -> 138 us
    pallas_call x1, Pallas kernels: 114 us -> 123 us  [layer(): pl.pallas_call(layer_kernel, out_shape=jax.ShapeDtypeStruct((128, 224), B...]
    pallas_call x1, Pallas kernels: 15.4 us -> 12.7 us  [attend(): pl.pallas_call(attend_kernel, out_shape=jax.ShapeDtypeStruct((4, 32, 512)...]
  transfers between devices with their start and end apart: 2 -> 2, of which waited for: 0 -> 0; matrix products, arithmetic and copies ran while one was open for 0% -> 0% of each run, Pallas kernels for 11% -> 9%
where the time goes in v6:
time: 145 us; the launch traced here: 143 us
  Pallas kernels  138 us (95%)
  starting transfers between devices  3.5 us (2%)
  local copies, waits for them, and re-layouts  1.74 us (1%)
    pallas_call x1, Pallas kernels, layer(): pl.pallas_call(layer_kernel, out_shape=jax.ShapeDtypeStruct((128, 224), B...  123 us
    pallas_call x1, Pallas kernels, attend(): pl.pallas_call(attend_kernel, out_shape=jax.ShapeDtypeStruct((4, 32, 512)...  12.7 us
    ppermute x2, starting transfers between devices, spread(): got.append(lax.ppermute(piece, 'dp', pairs))  3.5 us
  transfers between devices with their start and end apart: 2, of which 0 were waited for; matrix products, arithmetic and copies ran while one was open for 0% of the time, Pallas kernels for 9%

profile of v6, /device:TPU:1, one launch (start us, length us, event | category | flops | bytes accessed | tf_op | source)
XLA Modules:
  0.0 143.1 jit_solution(11809960350575570304)
XLA Ops:
  0.0 2.4 %shard_map.155 = (bf16[224,1280]{1,0:T(8,128)(2,1)}, bf16[224,1280]{1,0:T(8,128)(2,1)}) custom-call(bf16[224,2304]{1,0:T(8,128)(2,1)} %w_gate.3, bf16[224,2304]{1,0:T(8,128)(2,1)} %w_up.3), custom_call_target="tpu_custom_call" | custom-call | tf_op jit(solution)/shard_map/pallas_call | solution.py:711
  2.4 2.1 %collective-permute-start = (bf16[224,1280]{1,0:T(8,128)(2,1)}, bf16[224,1280]{1,0:T(8,128)(2,1)S(1)}, u32[]{:S(2)}, u32[]{:S(2)}) collective-permute-start(bf16[224,1280]{1,0:T(8,128)(2,1)} %get-tuple-element.7), channel_id=1, source_target_pairs={{0,64},{8,72},{16,80},{24,88},{32,96},{40,104},{48,112},{56,120},{... | collective-permute-start | bytes 1720328 | tf_op jit(solution)/shard_map/ppermute | solution.py:721
  4.5 0.0 copy-start.1
  4.5 0.0 copy-start.2
  4.5 1.4 collective-permute-start.1
  5.9 12.7 %shard_map.154.hv = bf16[4,32,512]{2,1,0:T(8,128)(2,1)} custom-call(s32[1,2,32]{2,1,0:T(2,128)} %table.1, s32[1,2]{1,0:T(1,128)} %hit.1, s32[1,2]{1,0:T(1,128)} %count.1, bf16[32,8192]{1,0:T(8,128)(2,1)} %q_lat.1, bf16[32,1024]{1,0:T(8,128)(2,1)} %q_rope.1, bf16[32,512]{1,0:T(8,128)(2,1)} %fresh_lat.1, bf16[32,64]{1,0:T(8,128)(2,1)} %fresh_rope.1, ...), custom_call_target="tpu_custom_call" | custom-call | flops 20000000000 | bytes 12582912 | tf_op jit(solution)/shard_map/pallas_call | solution.py:170
  18.6 0.0 copy-done.1
  18.6 0.1 copy.17.resid
  18.7 0.0 copy-done.2
  18.7 0.0 collective-permute-done.wgu1
  18.7 0.0 collective-permute-done.1.wgu3
  18.7 0.0 copy-start
  18.7 0.9 copy-done
  19.6 122.7 %shard_map.156 = bf16[128,224]{1,0:T(8,128)(2,1)S(1)} custom-call(bf16[4,32,512]{2,1,0:T(8,128)(2,1)S(1)} %copy-done, bf16[128,224]{1,0:T(8,128)(2,1)S(1)} %copy.17.resid, bf16[1,224]{1,0:T(2,128)(2,1)S(1)} %reshape.3.gain, bf16[224,2304]{1,0:T(8,128)(2,1)} %w_gate.3, bf16[224,2304]{1,0:T(8,128)(2,1)} %w_up.3, ...), custom_call_target="tpu_custom_call" | custom-call | tf_op jit(solution)/shard_map/pallas_call | solution.py:649
  142.3 0.7 copy.18
  (1 shorter events, 0.0 us)
Async XLA Ops:
  2.4 16.3 %collective-permute-start = (bf16[224,1280]{1,0:T(8,128)(2,1)}, bf16[224,1280]{1,0:T(8,128)(2,1)S(1)}, u32[]{:S(2)}, u32[]{:S(2)}) collective-permute-start(bf16[224,1280]{1,0:T(8,128)(2,1)} %get-tuple-element.7), channel_id=1, source_target_pairs={{0,64},{8,72},{16,80},{24,88},{32,96},{40,104},{48,112},{56,120},{... | collective-permute-start | bytes 1720328 | tf_op jit(solution)/shard_map/ppermute | solution.py:721
  4.5 14.0 %copy-start.1 = (bf16[128,224]{0,1:T(8,128)(2,1)S(1)}, bf16[128,224]{0,1:T(8,128)(2,1)}, u32[]{:S(2)}) copy-start(bf16[128,224]{0,1:T(8,128)(2,1)} %param.27) | copy-start | bytes 172036
  4.5 14.2 %copy-start.2 = (bf16[224]{0:T(256)(128)(2,1)S(1)}, bf16[224]{0:T(256)(128)(2,1)}, u32[]{:S(2)}) copy-start(bf16[224]{0:T(256)(128)(2,1)} %param.28) | copy-start | bytes 1348
  4.5 14.2 %collective-permute-start.1 = (bf16[224,1280]{1,0:T(8,128)(2,1)}, bf16[224,1280]{1,0:T(8,128)(2,1)S(1)}, u32[]{:S(2)}, u32[]{:S(2)}) collective-permute-start(bf16[224,1280]{1,0:T(8,128)(2,1)} %get-tuple-element.8), channel_id=1, source_target_pairs={{0,192},{8,200},{16,208},{24,216},{32,224},{40,232},{48,240},{56,2... | collective-permute-start | bytes 1720328 | tf_op jit(solution)/shard_map/ppermute | solution.py:721
  18.7 0.9 copy-start

commit v7 on v6

--- a/solution.py
+++ b/solution.py
@@ -375,27 +375,27 @@
         send(hv.at[lax.rem(x + k, X)], heads.at[z, x], x_of[k]) for k in (1, 2, 3)
     ]
 
-    wo_moves = [
-        send(
-            w_o.at[:, pl.ds(pl.multiple_of(lax.rem(x + k, X) * 512, 512), 512)],
-            wo.at[k],
-            x_of[k],
-        )
-        for k in (1, 2, 3)
-    ]
+    wo_moves = []
+
+    def move_heads(k):
+        there = pl.ds(pl.multiple_of(lax.rem(x + k, X) * 512, 512), 512)
+        wo_moves.append(send(w_o.at[:, there], wo.at[k], x_of[k]))
 
     def own_heads(sub):
         if sub:
             moved[sub].wait_recv()
         else:
             own_heads_copy.wait()
+        if sub == 0:
+            for k in (1, 2, 3):
+                move_heads(k)
 
     unit_moves = []
     seen = []
 
     def heads_arrived(zi):
         seen.append(zi)
-        if len(seen) == 2:
+        if len(seen) == 4:
             for src, dst in unit_blocks(lax.rem(x + 2, X)):
                 unit_moves.append(send(src, dst, x_of[2]))
 

time: 145 us -> 140 us (0.966)
  Pallas kernels: 138 us -> 133 us
    pallas_call x1, Pallas kernels: 123 us -> 119 us  [layer(): pl.pallas_call(layer_kernel, out_shape=jax.ShapeDtypeStruct((128, 224), B...]
  transfers between devices with their start and end apart: 2 -> 2, of which waited for: 0 -> 1; matrix products, arithmetic and copies ran while one was open for 0% -> 0% of each run, Pallas kernels for 9% -> 8%
where the time goes in v7:
time: 140 us; the launch traced here: 139 us
  Pallas kernels  133 us (95%)
  starting transfers between devices  3.5 us (2%)
  local copies, waits for them, and re-layouts  1.75 us (1%)
    pallas_call x1, Pallas kernels, layer(): pl.pallas_call(layer_kernel, out_shape=jax.ShapeDtypeStruct((128, 224), B...  119 us
    pallas_call x1, Pallas kernels, attend(): pl.pallas_call(attend_kernel, out_shape=jax.ShapeDtypeStruct((4, 32, 512)...  11.3 us
    ppermute x2, starting transfers between devices, spread(): got.append(lax.ppermute(piece, 'dp', pairs))  3.5 us
  transfers between devices with their start and end apart: 2, of which 1 were waited for; matrix products, arithmetic and copies ran while one was open for 0% of the time, Pallas kernels for 8%

profile of v7, /device:TPU:1, one launch (start us, length us, event | category | flops | bytes accessed | tf_op | source)
XLA Modules:
  0.0 138.8 jit_solution(8888675866148741418)
XLA Ops:
  0.0 2.4 %shard_map.155 = (bf16[224,1280]{1,0:T(8,128)(2,1)}, bf16[224,1280]{1,0:T(8,128)(2,1)}) custom-call(bf16[224,2304]{1,0:T(8,128)(2,1)} %w_gate.3, bf16[224,2304]{1,0:T(8,128)(2,1)} %w_up.3), custom_call_target="tpu_custom_call" | custom-call | tf_op jit(solution)/shard_map/pallas_call | solution.py:711
  2.4 2.1 %collective-permute-start = (bf16[224,1280]{1,0:T(8,128)(2,1)}, bf16[224,1280]{1,0:T(8,128)(2,1)S(1)}, u32[]{:S(2)}, u32[]{:S(2)}) collective-permute-start(bf16[224,1280]{1,0:T(8,128)(2,1)} %get-tuple-element.7), channel_id=1, source_target_pairs={{0,64},{8,72},{16,80},{24,88},{32,96},{40,104},{48,112},{56,120},{... | collective-permute-start | bytes 1720328 | tf_op jit(solution)/shard_map/ppermute | solution.py:721
  4.5 0.0 copy-start.1
  4.5 0.0 copy-start.2
  4.5 1.4 collective-permute-start.1
  5.9 11.3 %shard_map.154.hv = bf16[4,32,512]{2,1,0:T(8,128)(2,1)} custom-call(s32[1,2,32]{2,1,0:T(2,128)} %table.1, s32[1,2]{1,0:T(1,128)} %hit.1, s32[1,2]{1,0:T(1,128)} %count.1, bf16[32,8192]{1,0:T(8,128)(2,1)} %q_lat.1, bf16[32,1024]{1,0:T(8,128)(2,1)} %q_rope.1, bf16[32,512]{1,0:T(8,128)(2,1)} %fresh_lat.1, bf16[32,64]{1,0:T(8,128)(2,1)} %fresh_rope.1, ...), custom_call_target="tpu_custom_call" | custom-call | flops 20000000000 | bytes 12582912 | tf_op jit(solution)/shard_map/pallas_call | solution.py:170
  17.2 0.0 copy-done.1
  17.2 0.1 copy.17.resid
  17.3 0.0 copy-done.2
  17.3 0.0 collective-permute-done.wgu1
  17.3 0.6 collective-permute-done.1.wgu3
  17.9 0.0 copy-start
  17.9 0.9 copy-done
  18.8 119.2 %shard_map.156 = bf16[128,224]{1,0:T(8,128)(2,1)S(1)} custom-call(bf16[4,32,512]{2,1,0:T(8,128)(2,1)S(1)} %copy-done, bf16[128,224]{1,0:T(8,128)(2,1)S(1)} %copy.17.resid, bf16[1,224]{1,0:T(2,128)(2,1)S(1)} %reshape.3.gain, bf16[224,2304]{1,0:T(8,128)(2,1)} %w_gate.3, bf16[224,2304]{1,0:T(8,128)(2,1)} %w_up.3, ...), custom_call_target="tpu_custom_call" | custom-call | tf_op jit(solution)/shard_map/pallas_call | solution.py:649
  138.0 0.7 copy.18
  (1 shorter events, 0.0 us)
Async XLA Ops:
  2.4 14.9 %collective-permute-start = (bf16[224,1280]{1,0:T(8,128)(2,1)}, bf16[224,1280]{1,0:T(8,128)(2,1)S(1)}, u32[]{:S(2)}, u32[]{:S(2)}) collective-permute-start(bf16[224,1280]{1,0:T(8,128)(2,1)} %get-tuple-element.7), channel_id=1, source_target_pairs={{0,64},{8,72},{16,80},{24,88},{32,96},{40,104},{48,112},{56,120},{... | collective-permute-start | bytes 1720328 | tf_op jit(solution)/shard_map/ppermute | solution.py:721
  4.5 12.7 %copy-start.1 = (bf16[128,224]{0,1:T(8,128)(2,1)S(1)}, bf16[128,224]{0,1:T(8,128)(2,1)}, u32[]{:S(2)}) copy-start(bf16[128,224]{0,1:T(8,128)(2,1)} %param.27) | copy-start | bytes 172036
  4.5 12.8 %copy-start.2 = (bf16[224]{0:T(256)(128)(2,1)S(1)}, bf16[224]{0:T(256)(128)(2,1)}, u32[]{:S(2)}) copy-start(bf16[224]{0:T(256)(128)(2,1)} %param.28) | copy-start | bytes 1348
  4.5 13.4 %collective-permute-start.1 = (bf16[224,1280]{1,0:T(8,128)(2,1)}, bf16[224,1280]{1,0:T(8,128)(2,1)S(1)}, u32[]{:S(2)}, u32[]{:S(2)}) collective-permute-start(bf16[224,1280]{1,0:T(8,128)(2,1)} %get-tuple-element.8), channel_id=1, source_target_pairs={{0,192},{8,200},{16,208},{24,216},{32,224},{40,232},{48,240},{56,2... | collective-permute-start | bytes 1720328 | tf_op jit(solution)/shard_map/ppermute | solution.py:721
  17.9 0.9 copy-start

commit v8 on v7

--- a/solution.py
+++ b/solution.py
@@ -267,16 +267,16 @@
         sent.append(copy)
         return copy
 
-    def ring_gather(view, first, arrived):
+    def ring_gather(view, first, arrived, order=(0, 1, 2, 3)):
         got = {}
-        for sub in range(4):
+        for sub in order:
             first(sub)
             piece = view(z, sub)
             got["r", 0, sub] = send(piece, piece, right)
             got["l", 0, sub] = send(piece, piece, left)
         for hop in range(1, 4):
             zl, zr = lax.rem(z - hop + Z, Z), lax.rem(z + hop, Z)
-            for sub in range(4):
+            for sub in order:
                 got["r", hop - 1, sub].wait_recv()
                 if hop < 3 or sub < 2:
                     piece = view(zl, sub)
@@ -287,7 +287,7 @@
                     got["l", hop, sub] = send(piece, piece, left)
             arrived(zl)
             arrived(zr)
-        for sub in range(4):
+        for sub in order:
             got["r" if sub < 2 else "l", 3, sub].wait_recv()
         arrived(lax.rem(z + 4, Z))
 
@@ -622,7 +622,7 @@
             swap(3)
             add_swapped(2)
 
-    ring_gather(lambda zi, sub: hidden.at[zi, sub_rows(sub)], own_hidden, hidden_arrived)
+    ring_gather(lambda zi, sub: hidden.at[zi, sub_rows(sub)], own_hidden, hidden_arrived, (0, 2, 1, 3))
     add_swapped(3)
     halves = finish()
     for h, mlp in enumerate(halves):

time: 140 us -> 142 us (1.014)
  Pallas kernels: 133 us -> 135 us
    pallas_call x1, Pallas kernels: 11.3 us -> 14 us  [attend(): pl.pallas_call(attend_kernel, out_shape=jax.ShapeDtypeStruct((4, 32, 512)...]
  transfers between devices with their start and end apart: 2 -> 2, of which waited for: 1 -> 0; matrix products, arithmetic and copies ran while one was open for 0% -> 0% of each run, Pallas kernels for 8% -> 10%
where the time goes in v8:
time: 142 us; the launch traced here: 141 us
  Pallas kernels  135 us (95%)
  starting transfers between devices  3.5 us (2%)
  local copies, waits for them, and re-layouts  1.74 us (1%)
    pallas_call x1, Pallas kernels, layer(): pl.pallas_call(layer_kernel, out_shape=jax.ShapeDtypeStruct((128, 224), B...  119 us
    pallas_call x1, Pallas kernels, attend(): pl.pallas_call(attend_kernel, out_shape=jax.ShapeDtypeStruct((4, 32, 512)...  14 us
    ppermute x2, starting transfers between devices, spread(): got.append(lax.ppermute(piece, 'dp', pairs))  3.5 us
  transfers between devices with their start and end apart: 2, of which 0 were waited for; matrix products, arithmetic and copies ran while one was open for 0% of the time, Pallas kernels for 10%

profile of v8, /device:TPU:1, one launch (start us, length us, event | category | flops | bytes accessed | tf_op | source)
XLA Modules:
  0.0 140.5 jit_solution(8598922329156957304)
XLA Ops:
  0.0 2.4 %shard_map.155 = (bf16[224,1280]{1,0:T(8,128)(2,1)}, bf16[224,1280]{1,0:T(8,128)(2,1)}) custom-call(bf16[224,2304]{1,0:T(8,128)(2,1)} %w_gate.3, bf16[224,2304]{1,0:T(8,128)(2,1)} %w_up.3), custom_call_target="tpu_custom_call" | custom-call | tf_op jit(solution)/shard_map/pallas_call | solution.py:711
  2.4 2.1 %collective-permute-start = (bf16[224,1280]{1,0:T(8,128)(2,1)}, bf16[224,1280]{1,0:T(8,128)(2,1)S(1)}, u32[]{:S(2)}, u32[]{:S(2)}) collective-permute-start(bf16[224,1280]{1,0:T(8,128)(2,1)} %get-tuple-element.7), channel_id=1, source_target_pairs={{0,64},{8,72},{16,80},{24,88},{32,96},{40,104},{48,112},{56,120},{... | collective-permute-start | bytes 1720328 | tf_op jit(solution)/shard_map/ppermute | solution.py:721
  4.5 0.0 copy-start.1
  4.5 0.0 copy-start.2
  4.5 1.4 collective-permute-start.1
  5.9 14.0 %shard_map.154.hv = bf16[4,32,512]{2,1,0:T(8,128)(2,1)} custom-call(s32[1,2,32]{2,1,0:T(2,128)} %table.1, s32[1,2]{1,0:T(1,128)} %hit.1, s32[1,2]{1,0:T(1,128)} %count.1, bf16[32,8192]{1,0:T(8,128)(2,1)} %q_lat.1, bf16[32,1024]{1,0:T(8,128)(2,1)} %q_rope.1, bf16[32,512]{1,0:T(8,128)(2,1)} %fresh_lat.1, bf16[32,64]{1,0:T(8,128)(2,1)} %fresh_rope.1, ...), custom_call_target="tpu_custom_call" | custom-call | flops 20000000000 | bytes 12582912 | tf_op jit(solution)/shard_map/pallas_call | solution.py:170
  20.0 0.0 copy-done.1
  20.0 0.1 copy.17.resid
  20.1 0.0 copy-done.2
  20.1 0.0 collective-permute-done.wgu1
  20.1 0.0 collective-permute-done.1.wgu3
  20.1 0.0 copy-start
  20.1 0.9 copy-done
  21.0 118.8 %shard_map.156 = bf16[128,224]{1,0:T(8,128)(2,1)S(1)} custom-call(bf16[4,32,512]{2,1,0:T(8,128)(2,1)S(1)} %copy-done, bf16[128,224]{1,0:T(8,128)(2,1)S(1)} %copy.17.resid, bf16[1,224]{1,0:T(2,128)(2,1)S(1)} %reshape.3.gain, bf16[224,2304]{1,0:T(8,128)(2,1)} %w_gate.3, bf16[224,2304]{1,0:T(8,128)(2,1)} %w_up.3, ...), custom_call_target="tpu_custom_call" | custom-call | tf_op jit(solution)/shard_map/pallas_call | solution.py:649
  139.8 0.7 copy.18
  (1 shorter events, 0.0 us)
Async XLA Ops:
  2.4 17.7 %collective-permute-start = (bf16[224,1280]{1,0:T(8,128)(2,1)}, bf16[224,1280]{1,0:T(8,128)(2,1)S(1)}, u32[]{:S(2)}, u32[]{:S(2)}) collective-permute-start(bf16[224,1280]{1,0:T(8,128)(2,1)} %get-tuple-element.7), channel_id=1, source_target_pairs={{0,64},{8,72},{16,80},{24,88},{32,96},{40,104},{48,112},{56,120},{... | collective-permute-start | bytes 1720328 | tf_op jit(solution)/shard_map/ppermute | solution.py:721
  4.5 15.4 %copy-start.1 = (bf16[128,224]{0,1:T(8,128)(2,1)S(1)}, bf16[128,224]{0,1:T(8,128)(2,1)}, u32[]{:S(2)}) copy-start(bf16[128,224]{0,1:T(8,128)(2,1)} %param.27) | copy-start | bytes 172036
  4.5 15.5 %copy-start.2 = (bf16[224]{0:T(256)(128)(2,1)S(1)}, bf16[224]{0:T(256)(128)(2,1)}, u32[]{:S(2)}) copy-start(bf16[224]{0:T(256)(128)(2,1)} %param.28) | copy-start | bytes 1348
  4.5 15.6 %collective-permute-start.1 = (bf16[224,1280]{1,0:T(8,128)(2,1)}, bf16[224,1280]{1,0:T(8,128)(2,1)S(1)}, u32[]{:S(2)}, u32[]{:S(2)}) collective-permute-start(bf16[224,1280]{1,0:T(8,128)(2,1)} %get-tuple-element.8), channel_id=1, source_target_pairs={{0,192},{8,200},{16,208},{24,216},{32,224},{40,232},{48,240},{56,2... | collective-permute-start | bytes 1720328 | tf_op jit(solution)/shard_map/ppermute | solution.py:721
  20.1 0.9 copy-start
